TPU v7x, 32 devices: a whole 2x2x4 slice. The times are simulated.
32 devices in a mesh: grp: 2 (over y), sp: 16 (over z, x, core).
Axes of the slice: x: 2, y: 2, z: 4, core: 2. Of those that a mesh axis runs over, the one named last changes fastest.
Arguments:
- tokens: bfloat16 [128, 256, 512], P(('grp', 'sp')), may hold values from -6 to 6
- frame_slot: int32 [16, 8], P('grp'), may hold values from 0 to 7, each once within a row
- norm_gain: float32 [4, 512], replicated, may hold values from 0.1 to 1.9
- norm_shift: float32 [4, 512], replicated, may hold values from -4 to 4
- w_qkv: bfloat16 [2, 512, 1536], replicated, may hold values from -0.375 to 0.375
- w_out: bfloat16 [2, 512, 512], replicated, may hold values from -0.75 to 0.75
- w_up: bfloat16 [2, 512, 2048], replicated, may hold values from -0.25 to 0.25
- b_up: float32 [2, 2048], replicated, may hold values from -4 to 4
- w_down: bfloat16 [2, 2048, 512], replicated, may hold values from -0.125 to 0.125
- b_down: float32 [2, 512], replicated, may hold values from -4 to 4
- cotangent: bfloat16 [128, 256, 512], P(('grp', 'sp')), may hold values from -6 to 6
Outputs:
- output: bfloat16 [128, 256, 512], P(('grp', 'sp'))
- grad_tokens: bfloat16 [128, 256, 512], P(('grp', 'sp'))
- grad_norm_gain: float32 [4, 512], P(None, 'sp')
- grad_norm_shift: float32 [4, 512], P(None, 'sp')
- grad_w_qkv: float32 [2, 512, 1536], P(None, 'sp')
- grad_w_out: float32 [2, 512, 512], P(None, 'sp')
- grad_w_up: float32 [2, 512, 2048], P(None, 'sp')
- grad_b_up: float32 [2, 2048], P(None, 'sp')
- grad_w_down: float32 [2, 2048, 512], P(None, 'sp')
- grad_b_down: float32 [2, 512], P(None, 'sp')
Inputs may be any that keep to these rules, and one draw needn't show every extreme that they name: `frame_slot`: each row names every slot of a group once; slots 0 to 5 are the video's time steps, the others are images.
All inputs are finite; a program needn't handle non-finite values.
Results may differ from a plain program's by a relative error of at most 0.028.
Values may be sent and summed in bfloat16 or wider, within the bound.
No kernel may reach another device: no remote copies, remote signals or barrier semaphores. Data moves between devices by JAX's collectives and lax.ppermute only.
A program may use at most 192 MiB of HBM per device.

v0:
```python
import functools

import jax
import jax.numpy as jnp
from jax import lax
from jax.experimental import pallas as pl
from jax.experimental.pallas import tpu as pltpu
from jax.sharding import PartitionSpec as P

HEADS = 8
HEAD = 64
VIDEO_STEPS = 6
GROUP_FRAMES = 8
NORM_EPS = 1e-05
TILE = 512
STEP = 1024
SCALE = HEAD**-0.5
TANH_A = 0.7978845608028654
TANH_B = TANH_A * 0.044715
PAIRS = [(t, s) for t in range(VIDEO_STEPS) for s in range(t + 1)]
F32 = jnp.float32
BF16 = jnp.bfloat16
MIB = 1024 * 1024
ROWS = -1
COST = 1.15e9 * 0.02
TAIL = ("q", "m", "bu", "q", "m", "bu", "q", "bu", "q", "bu", "q")
LIMIT1 = 52
LIMIT2 = 24


def dot(left, right):
    return jnp.dot(left, right, preferred_element_type=F32)


def dot_nt(left, right):
    return lax.dot_general(left, right, (((1,), (1,)), ((), ())), preferred_element_type=F32)


def dot_tn(left, right):
    return lax.dot_general(left, right, (((0,), (0,)), ((), ())), preferred_element_type=F32)


def norm(rows, gain, shift):
    centred = rows - jnp.mean(rows, axis=-1, keepdims=True)
    inv = lax.rsqrt(jnp.mean(centred * centred, axis=-1, keepdims=True) + NORM_EPS)
    unit = centred * inv
    return unit * gain + shift, unit, inv


def norm_back(grad, unit, inv, gain):
    grad_unit = grad * gain
    mean_grad = jnp.mean(grad_unit, axis=-1, keepdims=True)
    mean_both = jnp.mean(grad_unit * unit, axis=-1, keepdims=True)
    return inv * (grad_unit - mean_grad - unit * mean_both)


def column_sum(rows):
    return jnp.sum(rows, axis=0, keepdims=True)


def gelu_pair(u):
    square = u * u
    sigma = 0.5 + 0.5 * jnp.tanh(u * (TANH_A + TANH_B * square))
    act = u * sigma
    slope = sigma + act * (1.0 - sigma) * (2.0 * TANH_A + 6.0 * TANH_B * square)
    return act.astype(BF16), slope.astype(BF16)


def head_mask(lanes, which):
    lane = lax.broadcasted_iota(jnp.int32, lanes.shape, 1)
    return (lane < HEAD) if which == 0 else (lane >= HEAD)


def qkv_rows(normed, weight):
    out = []
    for part in range(3):
        piece = dot(normed, weight[:, part * TILE : (part + 1) * TILE])
        if part == 0:
            out.append(piece.astype(BF16) * BF16(SCALE))
        else:
            out.append(piece.astype(BF16))
    return out


def mlp_forward(normed, w_up, b_up, w_down, rows, act_ref, slope_ref):
    chunks = w_up.shape[1] // STEP
    up = lambda j: dot(normed, w_up[:, j * STEP : (j + 1) * STEP])
    total = None
    u = up(0)
    for j in range(chunks):
        cols = slice(j * STEP, (j + 1) * STEP)
        later = up(j + 1) if j + 1 < chunks else None
        act, slope = gelu_pair(u + b_up[0:1, cols])
        act_ref[rows, cols] = act
        slope_ref[rows, cols] = slope
        piece = dot(act, w_down[cols, :])
        total = piece if total is None else total + piece
        u = later
    return total


def mlp_backward(grad_low, w_up, w_down, rows, slope_ref, du_ref):
    chunks = w_up.shape[1] // STEP
    down = lambda j: dot_nt(grad_low, w_down[j * STEP : (j + 1) * STEP, :])
    total = None
    sums = []
    da = down(0)
    for j in range(chunks):
        cols = slice(j * STEP, (j + 1) * STEP)
        later = down(j + 1) if j + 1 < chunks else None
        du = (da * slope_ref[rows, cols].astype(F32)).astype(BF16)
        du_ref[rows, cols] = du
        sums.append(column_sum(du.astype(F32)))
        piece = dot_nt(du, w_up[:, cols])
        total = piece if total is None else total + piece
        da = later
    return total, [x[:, k : k + TILE] for x in sums for k in range(0, STEP, TILE)]


def add_small(small_ref, values, first):
    for i, value in enumerate(values):
        row = slice(i, i + 1) if i < 4 else slice(i, i + 1)
        if value is None:
            continue
        if first:
            small_ref[row, :] = value
        else:
            small_ref[row, :] += value


def rows_at(index, count):
    return pl.ds(pl.multiple_of(index * count, count), count)


def half_rows(part, half):
    return pl.ds(pl.multiple_of(part * half, half), half)


def space_forward_kernel(
    tok_hbm, params_ref, wqkv_hbm, wout_hbm, wup_hbm, wdown_hbm,
    keep_ref, send_ref, h0_hbm, qkv_hbm, lse_ref, o_hbm, xa_hbm, h1_hbm, act_hbm, slope_hbm,
    tok_ref, wqkv_ref, wout_ref, wup_ref, wdown_ref, h0_scr, qkv_scr, o_scr, xa_scr, h1_scr, act_scr,
    slope_scr, x1_scr, in_sems, out_sems,
):
    pairs = [
        (tok_hbm, tok_ref), (wqkv_hbm.at[0], wqkv_ref), (wout_hbm.at[0], wout_ref),
        (wup_hbm.at[0], wup_ref), (wdown_hbm.at[0], wdown_ref),
    ]
    copies = [pltpu.make_async_copy(src, dst, in_sems.at[i]) for i, (src, dst) in enumerate(pairs)]
    for copy in copies[:2]:
        copy.start()
    gain_ref, shift_ref = params_ref.at[0:4, 0:TILE], params_ref.at[4:8, 0:TILE]
    part = lax.rem(lax.axis_index("sp"), 2)
    frames, rows = tok_ref.shape[0], tok_ref.shape[1]
    half = rows // 2
    lane = lax.broadcasted_iota(jnp.int32, (rows, 128), 1)
    places = (
        (h0_scr, h0_hbm), (qkv_scr, qkv_hbm), (o_scr, o_hbm), (xa_scr, xa_hbm), (h1_scr, h1_hbm),
        (act_scr, act_hbm), (slope_scr, slope_hbm),
    )

    def spills(f):
        now = lax.rem(f, 2)
        return [
            pltpu.make_async_copy(scr.at[now], hbm.at[rows_at(f, rows)], out_sems.at[7 * now + i])
            for i, (scr, hbm) in enumerate(places)
        ]

    def await_first(f, *which):
        @pl.when(f == 0)
        def _():
            for i in which:
                copies[i].wait()

    copies[0].wait()
    for copy in copies[2:]:
        copy.start()

    @pl.loop(0, frames)
    def _(f):
        now = lax.rem(f, 2)
        spill = spills(f)

        @pl.when(f >= 2)
        def _():
            for copy in spills(f - 2):
                copy.wait()

        x0 = tok_ref[f].astype(F32)
        h0 = norm(x0, gain_ref[0:1, :], shift_ref[0:1, :])[0].astype(BF16)
        h0_scr[now] = h0
        spill[0].start()
        await_first(f, 1)
        q, k, v = qkv_rows(h0, wqkv_ref)
        qkv_scr[now, :, 0:TILE] = q
        qkv_scr[now, :, TILE : 2 * TILE] = k
        qkv_scr[now, :, 2 * TILE :] = v
        spill[1].start()
        lse_all = jnp.zeros((rows, 128), F32)
        mixed = []
        for pair in range(HEADS // 2):
            cols = slice(pair * 128, (pair + 1) * 128)
            qp, kp, vp = q[:, cols], k[:, cols], v[:, cols]
            zero = jnp.zeros_like(qp)
            mask = head_mask(qp, 0)
            s = dot_nt(jnp.concatenate([jnp.where(mask, qp, zero), jnp.where(mask, zero, qp)], axis=0), kp)
            top = jnp.max(s, axis=-1, keepdims=True)
            p = jnp.exp(s - top)
            total = jnp.sum(p, axis=-1, keepdims=True)
            both = dot(p.astype(BF16), vp) * (1.0 / total)
            lse = top + jnp.log(total)
            lse_all = jnp.where(lane == 2 * pair, lse[:rows], lse_all)
            lse_all = jnp.where(lane == 2 * pair + 1, lse[rows:], lse_all)
            mixed.append(jnp.where(mask, both[:rows], both[rows:]).astype(BF16))
        lse_ref[f] = jnp.transpose(lse_all)[0:HEADS, :]
        o = jnp.concatenate(mixed, axis=1)
        o_scr[now] = o
        spill[2].start()
        await_first(f, 2)
        xa = x0 + dot(o, wout_ref[...])
        xa_scr[now] = xa
        spill[3].start()
        h1 = norm(xa, gain_ref[1:2, :], shift_ref[1:2, :])[0].astype(BF16)
        h1_scr[now] = h1
        spill[4].start()
        await_first(f, 3, 4)
        branch = mlp_forward(
            h1, wup_ref, params_ref.at[8:9], wdown_ref, slice(None), act_scr.at[now], slope_scr.at[now]
        )
        spill[5].start()
        spill[6].start()
        x1_scr[...] = xa + branch + params_ref[10:11, 0:TILE]
        keep_ref[f] = x1_scr[half_rows(part, half), :].astype(BF16)
        send_ref[f] = x1_scr[half_rows(1 - part, half), :].astype(BF16)

    for f in (frames - 2, frames - 1):
        for copy in spills(jnp.int32(f)):
            copy.wait()


def lane_heads(dtype):
    c = lax.broadcasted_iota(jnp.int32, (TILE, 128), 0)
    h = lax.broadcasted_iota(jnp.int32, (TILE, 128), 1)
    return (c // HEAD == h).astype(dtype)


def slot_places(slots_ref, where_scr, frames):
    sp = lax.axis_index("sp")
    group = (sp * frames) // GROUP_FRAMES
    part = lax.rem(sp, GROUP_FRAMES // frames)
    for t in range(GROUP_FRAMES):
        where_scr[slots_ref[group, t]] = lax.rem(t + GROUP_FRAMES - part * frames, GROUP_FRAMES)


def time_scores(q, k, spread):
    parts = []
    for t, s in PAIRS:
        parts.append((q[t] * k[s]).astype(BF16))
    return dot(jnp.concatenate(parts, axis=0), spread)


def time_probs(scores, count):
    blocks = [scores[i * count : (i + 1) * count] for i in range(len(PAIRS))]
    probs = []
    at = 0
    for t in range(VIDEO_STEPS):
        mine = blocks[at : at + t + 1]
        at += t + 1
        top = functools.reduce(jnp.maximum, mine)
        raw = [jnp.exp(b - top) for b in mine]
        inv = 1.0 / functools.reduce(lambda a, b: a + b, raw)
        probs.extend([r * inv for r in raw])
    return probs


def split_slots(rows):
    count = rows.shape[0] // GROUP_FRAMES
    return [rows[s * count : (s + 1) * count].astype(F32) for s in range(GROUP_FRAMES)]


def time_forward_kernel(
    slots_ref, keep_ref, recv_ref, cot_ref, cotr_ref, params_ref,
    wqkv_hbm, wout_hbm, wup_hbm, wdown_hbm,
    own_ref, send_ref, x_ref, h2_ref, qkv_ref, o_ref, h3_ref, act_ref, du_ref, gr_ref, dxb_ref,
    small_ref, wqkv_ref, wout_ref,
    where_scr, both_scr, slope_scr, wup_ref, wdown_ref, in_sems,
):
    pairs = [(wqkv_hbm, wqkv_ref), (wout_hbm, wout_ref), (wup_hbm, wup_ref), (wdown_hbm, wdown_ref)]
    copies = [pltpu.make_async_copy(src.at[1], dst, in_sems.at[i]) for i, (src, dst) in enumerate(pairs)]
    for copy in copies:
        copy.start()
    gain_ref, shift_ref = params_ref.at[0:4, 0:TILE], params_ref.at[4:8, 0:TILE]
    frames, half = keep_ref.shape[0], keep_ref.shape[1]
    part = lax.rem(lax.axis_index("sp"), GROUP_FRAMES // frames)
    slot_places(slots_ref, where_scr, frames)
    small_ref[...] = jnp.zeros_like(small_ref)
    both_scr[0:frames] = keep_ref[...]
    both_scr[frames:] = recv_ref[...]
    spread = lane_heads(BF16)
    steps = 4
    count = half // steps
    step_rows = count * GROUP_FRAMES

    def await_first(i, *which):
        @pl.when(i == 0)
        def _():
            for w in which:
                copies[w].wait()

    @pl.loop(0, steps)
    def _(i):
        span = rows_at(i, step_rows)
        place = rows_at(i, count)
        x_low = jnp.concatenate([both_scr[where_scr[s], place] for s in range(GROUP_FRAMES)], axis=0)
        x_ref[span, :] = x_low
        x = x_low.astype(F32)
        h2 = norm(x, gain_ref[2:3, :], shift_ref[2:3, :])[0].astype(BF16)
        h2_ref[span, :] = h2
        await_first(i, 0)
        q, k, v = qkv_rows(h2, wqkv_ref)
        qkv_ref[span, 0:TILE] = q
        qkv_ref[span, TILE : 2 * TILE] = k
        qkv_ref[span, 2 * TILE :] = v
        qs, ks, vs = split_slots(q), split_slots(k), split_slots(v)
        probs = time_probs(time_scores(qs, ks, spread), count)
        wide = dot_nt(jnp.concatenate([p.astype(BF16) for p in probs], axis=0), spread)
        mixed = []
        at = 0
        for t in range(VIDEO_STEPS):
            total = None
            for s in range(t + 1):
                piece = wide[at * count : (at + 1) * count] * vs[s]
                total = piece if total is None else total + piece
                at += 1
            mixed.append(total)
        mixed.extend(vs[VIDEO_STEPS:])
        o = jnp.concatenate([m.astype(BF16) for m in mixed], axis=0)
        o_ref[span, :] = o
        await_first(i, 1)
        xb = x + dot(o, wout_ref[...]).astype(BF16).astype(F32)
        h3, unit, inv = norm(xb, gain_ref[3:4, :], shift_ref[3:4, :])
        h3 = h3.astype(BF16)
        h3_ref[span, :] = h3
        slope = slope_scr
        await_first(i, 2, 3)
        branch = mlp_forward(h3, wup_ref, params_ref.at[9:10], wdown_ref, span, act_ref, SpanView(slope))
        out = (xb + branch + params_ref[11:12, 0:TILE]).astype(BF16)
        for s in range(GROUP_FRAMES):
            both_scr[where_scr[s], place] = out[s * count : (s + 1) * count]
        grad_low = jnp.concatenate(
            [cot_slot(cot_ref, cotr_ref, where_scr[s], part * half + i * count, count) for s in range(GROUP_FRAMES)],
            axis=0,
        )
        gr_ref[span, :] = grad_low
        grad = grad_low.astype(F32)
        dh, sums = mlp_backward(grad_low, wup_ref, wdown_ref, span, SpanView(slope), du_ref)
        add_small(small_ref, [column_sum(dh * unit), column_sum(dh), column_sum(grad), None] + sums, False)
        dxb_ref[span, :] = grad + norm_back(dh, unit, inv, gain_ref[3:4, :])

    own_ref[...] = both_scr[0:frames]
    send_ref[...] = both_scr[frames:]


class SpanView:
    def __init__(self, ref):
        self.ref = ref

    def __getitem__(self, index):
        return self.ref[:, index[1]]

    def __setitem__(self, index, value):
        self.ref[:, index[1]] = value


def cot_slot(cot_ref, cotr_ref, frame, start, count):
    frames = cot_ref.shape[0]
    places = pl.ds(pl.multiple_of(start, count), count)
    mine = cot_ref[lax.rem(frame, frames), places, :]
    other = cotr_ref[lax.rem(frame, frames), places, :]
    return jnp.where(frame < frames, mine, other)


def time_backward_kernel(
    slots_ref, x_ref, qkv_ref, dxb_ref, params_ref, wqkv_ref, wout_ref,
    own_ref, send_ref, ar_ref, dqkv_ref, small_ref,
    where_scr, both_scr,
):
    frames, half = own_ref.shape[0], own_ref.shape[1]
    slot_places(slots_ref, where_scr, frames)
    small_ref[...] = jnp.zeros_like(small_ref)
    spread = lane_heads(BF16)
    steps = 4
    count = half // steps
    step_rows = count * GROUP_FRAMES
    gain = params_ref[2:3, 0:TILE]

    @pl.loop(0, steps)
    def _(i):
        span = rows_at(i, step_rows)
        place = rows_at(i, count)
        dxb = dxb_ref[span, :]
        ar = dxb.astype(BF16)
        ar_ref[span, :] = ar
        do = split_slots(dot_nt(ar, wout_ref[...]).astype(BF16))
        qs = split_slots(qkv_ref[span, 0:TILE])
        ks = split_slots(qkv_ref[span, TILE : 2 * TILE])
        vs = split_slots(qkv_ref[span, 2 * TILE :])
        probs = time_probs(time_scores(qs, ks, spread), count)
        dps = time_scores(do, vs, spread)
        dps = [dps[j * count : (j + 1) * count] for j in range(len(PAIRS))]
        dss = []
        at = 0
        for t in range(VIDEO_STEPS):
            centre = functools.reduce(
                lambda a, b: a + b, [probs[at + s] * dps[at + s] for s in range(t + 1)]
            )
            dss.extend([probs[at + s] * (dps[at + s] - centre) for s in range(t + 1)])
            at += t + 1
        wide_p = dot_nt(jnp.concatenate([p.astype(BF16) for p in probs], axis=0), spread)
        wide_ds = dot_nt(jnp.concatenate([d.astype(BF16) for d in dss], axis=0), spread)
        dq = [None] * GROUP_FRAMES
        dk = [None] * GROUP_FRAMES
        dv = [None] * GROUP_FRAMES

        def add(table, index, piece):
            table[index] = piece if table[index] is None else table[index] + piece

        for j, (t, s) in enumerate(PAIRS):
            rows = slice(j * count, (j + 1) * count)
            add(dq, t, wide_ds[rows] * ks[s])
            add(dk, s, wide_ds[rows] * qs[t])
            add(dv, s, wide_p[rows] * do[t])
        for t in range(VIDEO_STEPS, GROUP_FRAMES):
            dq[t] = jnp.zeros_like(do[t])
            dk[t] = jnp.zeros_like(do[t])
            dv[t] = do[t]
        dq = jnp.concatenate([(d * SCALE).astype(BF16) for d in dq], axis=0)
        dk = jnp.concatenate([d.astype(BF16) for d in dk], axis=0)
        dv = jnp.concatenate([d.astype(BF16) for d in dv], axis=0)
        dqkv_ref[span, 0:TILE] = dq
        dqkv_ref[span, TILE : 2 * TILE] = dk
        dqkv_ref[span, 2 * TILE :] = dv
        dh = dot_nt(dqkv_ref[span, :], wqkv_ref[...])
        unit, inv = norm(x_ref[span, :].astype(F32), gain, params_ref[6:7, 0:TILE])[1:]
        add_small(small_ref, [column_sum(dh * unit), column_sum(dh)], False)
        dxp = norm_back(dh, unit, inv, gain).astype(BF16).astype(F32)
        dx1 = (dxb + dxp).astype(BF16)
        for s in range(GROUP_FRAMES):
            both_scr[where_scr[s], place] = dx1[s * count : (s + 1) * count]

    own_ref[...] = both_scr[0:frames]
    send_ref[...] = both_scr[frames:]


def space_mlp_back_kernel(
    gr_ref, xa_ref, slope_ref, params_ref, wup_ref, wdown_ref,
    du_ref, dxa_ref, ar_ref, small_ref,
):
    small_ref[...] = jnp.zeros_like(small_ref)
    rows = 256
    gain = params_ref[1:2, 0:TILE]

    @pl.loop(0, gr_ref.shape[0] // rows)
    def _(f):
        span = rows_at(f, rows)
        grad_low = gr_ref[span, :]
        grad = grad_low.astype(F32)
        dh, sums = mlp_backward(grad_low, wup_ref.at[0], wdown_ref.at[0], span, slope_ref, du_ref)
        unit, inv = norm(xa_ref[span, :], gain, params_ref[5:6, 0:TILE])[1:]
        add_small(small_ref, [column_sum(dh * unit), column_sum(dh), column_sum(grad), None] + sums, False)
        dxa = grad + norm_back(dh, unit, inv, gain)
        dxa_ref[span, :] = dxa
        ar_ref[span, :] = dxa.astype(BF16)


def head_picker():
    h = lax.broadcasted_iota(jnp.int32, (HEADS, TILE), 0)
    c = lax.broadcasted_iota(jnp.int32, (HEADS, TILE), 1)
    return (c // HEAD == h).astype(BF16)


def attn_back_frame(f, ar_ref, qkv_ref, lse_ref, o_ref, wout_ref, pick, dqkv_ref):
    rows = lse_ref.shape[2]
    span = rows_at(f, rows)
    do = dot_nt(ar_ref[span, :], wout_ref[0]).astype(BF16)
    both = do.astype(F32) * o_ref[span, :].astype(F32)
    high = both.astype(BF16)
    rest = (both - high.astype(F32)).astype(BF16)
    centre = dot_nt(pick, high) + dot_nt(pick, rest)
    for pair in range(HEADS // 2):
        qp = qkv_ref[span, pair * 128 : (pair + 1) * 128]
        kp = qkv_ref[span, TILE + pair * 128 : TILE + (pair + 1) * 128]
        vp = qkv_ref[span, 2 * TILE + pair * 128 : 2 * TILE + (pair + 1) * 128]
        dop = do[:, pair * 128 : (pair + 1) * 128]
        zero = jnp.zeros_like(kp)
        mask = head_mask(kp, 0)
        st = dot_nt(jnp.concatenate([jnp.where(mask, kp, zero), jnp.where(mask, zero, kp)], axis=0), qp)
        dpt = dot_nt(jnp.concatenate([jnp.where(mask, vp, zero), jnp.where(mask, zero, vp)], axis=0), dop)
        pts, dsts, dqs = [], [], []
        for e in range(2):
            row = slice(2 * pair + e, 2 * pair + e + 1)
            keys = slice(e * rows, (e + 1) * rows)
            pt = jnp.exp(st[keys] - lse_ref[f, row, :])
            dst = (pt * (dpt[keys] - centre[row, :])).astype(BF16)
            pts.append(pt.astype(BF16))
            dsts.append(dst)
            dqs.append(dot_tn(dst, kp) * SCALE)
        dk = dot(jnp.concatenate(dsts, axis=0), qp)
        dv = dot(jnp.concatenate(pts, axis=0), dop)
        values = (
            jnp.where(mask, dqs[0], dqs[1]),
            jnp.where(mask, dk[:rows], dk[rows:]),
            jnp.where(mask, dv[:rows], dv[rows:]),
        )
        for index, value in enumerate(values):
            at = index * TILE + pair * 128
            dqkv_ref[span, at : at + 128] = value.astype(BF16)


def space_attn_back_kernel(ar_ref, qkv_ref, lse_ref, o_ref, wout_ref, dqkv_ref):
    pick = head_picker()

    @pl.loop(0, lse_ref.shape[0])
    def _(f):
        attn_back_frame(f, ar_ref, qkv_ref, lse_ref, o_ref, wout_ref, pick, dqkv_ref)


def qkv_weights_kernel(order, dqkv_ref, h_ref, keep_ref, send_ref):
    size = h_ref.shape[1] // lax.axis_size("sp")
    turned_columns(h_ref, dqkv_ref, 3, 0, 3 * size, size, order, keep_ref, send_ref)


def finish_kernel(
    dqkv_ref, tok_ref, dxa_ref, own_ref, recv_ref, params_ref, wqkv_ref, small1_ref,
    small2_ref, small3_ref, gtok_ref, out_ref, small_ref, sums_scr,
):
    part = lax.rem(lax.axis_index("sp"), 2)
    frames, half = own_ref.shape[0], own_ref.shape[1]
    rows = 2 * half
    gain = params_ref[0:1, 0:TILE]
    sums_scr[...] = jnp.zeros_like(sums_scr)

    @pl.loop(0, frames)
    def _(f):
        span = rows_at(f, rows)
        out_ref[f, half_rows(part, half), :] = own_ref[f]
        out_ref[f, half_rows(1 - part, half), :] = recv_ref[f]
        dh = dot_nt(dqkv_ref[span, :], wqkv_ref[0])
        unit, inv = norm(tok_ref[f].astype(F32), gain, params_ref[4:5, 0:TILE])[1:]
        add_small(sums_scr, [column_sum(dh * unit), column_sum(dh)], False)
        gtok_ref[f] = (dxa_ref[span, :] + norm_back(dh, unit, inv, gain)).astype(BF16)

    small = jnp.concatenate([sums_scr[...], small1_ref[...], small2_ref[...], small3_ref[...]], axis=0)
    small_ref[...] = small.astype(BF16)


def place_of(block, order, sp):
    bits = len(order)
    mixed = jnp.bitwise_xor(block, sp)
    slot = jnp.int32(0)
    for i, b in enumerate(order):
        bit = jnp.bitwise_and(lax.shift_right_logical(mixed, jnp.int32(b)), 1)
        slot = slot + lax.shift_left(bit, jnp.int32(bits - 1 - i))
    return slot


class Place:
    def __init__(self, base, rows, at):
        self.base, self.rows, self.at = base, rows, at


def put_blocks(result, first, size, place, order, keep_ref, send_ref):
    sp = lax.axis_index("sp")
    part = lax.rem(sp, 2)
    low = result.astype(BF16)
    for j in range(result.shape[0] // (2 * size)):
        even = low[2 * j * size : (2 * j + 1) * size]
        odd = low[(2 * j + 1) * size : (2 * j + 2) * size]
        slot = place_of(first + 2 * j, order[1:], sp)
        rows = pl.ds(pl.multiple_of(place.base + slot * place.rows + place.at, 16), size)
        keep_ref[rows, :] = jnp.where(part == 0, even, odd)
        send_ref[rows, :] = jnp.where(part == 0, odd, even)


def turned_columns(h_ref, wide_ref, chunks, base, rows, size, order, keep_ref, send_ref):
    turned = jnp.transpose(h_ref[...])
    for j in range(chunks):
        result = dot(turned, wide_ref[:, j * TILE : (j + 1) * TILE])
        put_blocks(result, jnp.int32(0), size, Place(base, rows, j * size), order, keep_ref, send_ref)


def put_up(h_ref, du_ref, base, rows, order, keep_ref, send_ref):
    size = h_ref.shape[1] // lax.axis_size("sp")
    turned_columns(h_ref, du_ref, du_ref.shape[1] // TILE, base, rows, size, order, keep_ref, send_ref)


def put_down(act_ref, gr_ref, base, order, keep_ref, send_ref):
    size = act_ref.shape[1] // lax.axis_size("sp")
    for j in range(act_ref.shape[1] // TILE):
        down = dot_tn(act_ref[:, j * TILE : (j + 1) * TILE], gr_ref[...])
        put_blocks(down, jnp.int32(j * (TILE // size)), size, Place(base, size, 0), order, keep_ref, send_ref)


def mlp_weights_kernel(orders, h_ref, du_ref, act_ref, gr_ref, keep_ref, send_ref):
    sp_size = lax.axis_size("sp")
    rows = du_ref.shape[1] // TILE * (h_ref.shape[1] // sp_size)
    put_up(h_ref, du_ref, 0, rows, orders[0], keep_ref, send_ref)
    put_down(act_ref, gr_ref, sp_size // 2 * rows, orders[1], keep_ref, send_ref)


def down_weights_kernel(order, act_ref, own_ref, recv_ref, gr_ref, keep_ref, send_ref):
    part = lax.rem(lax.axis_index("sp"), 2)
    frames, half = own_ref.shape[0], own_ref.shape[1]
    for f in range(frames):
        base = f * 2 * half
        gr_ref[pl.ds(pl.multiple_of(base + part * half, half), half), :] = own_ref[f]
        gr_ref[pl.ds(pl.multiple_of(base + (1 - part) * half, half), half), :] = recv_ref[f]
    put_down(act_ref, gr_ref, 0, order, keep_ref, send_ref)


def up_weights_kernel(order, h_ref, du_ref, o_ref, ar_ref, keep_ref, send_ref):
    size = h_ref.shape[1] // lax.axis_size("sp")
    at = du_ref.shape[1] // TILE * size
    put_up(h_ref, du_ref, 0, at + size, order, keep_ref, send_ref)
    out = dot_tn(o_ref[...], ar_ref[...])
    put_blocks(out, jnp.int32(0), size, Place(0, at + size, at), order, keep_ref, send_ref)


def attn_weights_kernel(order, h_ref, dqkv_ref, o_ref, ar_ref, keep_ref, send_ref):
    size = h_ref.shape[1] // lax.axis_size("sp")
    turned_columns(h_ref, dqkv_ref, 3, 0, 4 * size, size, order, keep_ref, send_ref)
    out = dot_tn(o_ref[...], ar_ref[...])
    put_blocks(out, jnp.int32(0), size, Place(0, 4 * size, 3 * size), order, keep_ref, send_ref)


def in_pieces(rows, body):
    piece = next(p for p in (128, 96, 80, 64, 48, 32, 16, 8) if rows % p == 0)
    if rows <= 2 * piece:
        for start in range(0, rows, piece):
            body(start, piece)
    else:

        @pl.loop(0, rows // piece)
        def _(i):
            body(pl.multiple_of(i * piece, 8), piece)


def fold_kernel(moves, count, *refs):
    outs = refs[2 * count :]
    row_half = lax.rem(lax.axis_index("grp"), 2)

    def add(keep, recv, at, rows, places):
        def body(start, piece):
            span = pl.ds(pl.multiple_of(at + start, 8), piece)
            total = keep[span, :] + recv[span, :]
            for ref, to in places:
                ref[pl.ds(pl.multiple_of(to + start, 8), piece), :] = total

        in_pieces(rows, body)

    for source, at, rows, slots, targets, to, split in moves:
        keep, recv = refs[2 * source], refs[2 * source + 1]
        if split == "none":
            add(keep, recv, at, rows, [(outs[target], to) for target in targets])
        elif split == "slots":
            half = rows // 2
            for part, target in enumerate(targets):
                add(keep, recv, at + part * half, half, [(outs[target], to)])
        else:
            half = rows // (2 * slots)
            for slot in range(slots):
                for part, target in enumerate(targets):
                    side = row_half if part == 0 else 1 - row_half
                    add(keep, recv, at + 2 * slot * half + side * half, half, [(outs[target], to + slot * half)])


class Group:
    def __init__(self, sizes, segments, apart=False):
        grp_size, sp_size = sizes
        bits = sp_size.bit_length() - 1
        grp_bits = grp_size.bit_length() - 1
        names = tuple(segments)
        self.halved = grp_bits > 0 and all(
            whole or (height // 2) % 16 == 0 for height, whole, path in segments.values()
        )
        self.segments = {}
        self.state = {}
        for name, (height, whole, path) in segments.items():
            path = [step for step in path if step != ROWS or self.halved] + list(range(4, bits))
            self.segments[name] = (height, whole, path)
            self.state[name] = [sp_size // 2, 1]
        self.stages = []
        for i in range(bits + (1 if self.halved else 0)):
            entries = {}
            for name in names:
                key = (self.segments[name][2][i], name if apart and i == 0 else None)
                entries.setdefault(key, []).append(name)
            stage = []
            for (step, _), who in entries.items():
                stage.append(("grp", grp_size, 0, who, "rows") if step == ROWS else ("sp", sp_size, step, who, "slots"))
            self.stages.append(stage)
        for b in range(1 if self.halved else 0, grp_bits):
            self.stages.append([("grp", grp_size, b, names, "none")])
        if self.halved:
            self.stages.append([("grp", grp_size, 0, names, "none")])
        self.stage = 0
        self.keeps, self.recvs = [], []

    def beside(self, other):
        group = Group.__new__(Group)
        group.halved, group.stage = self.halved, self.stage
        group.segments = {**self.segments, **other.segments}
        group.state = {**self.state, **other.state}
        group.keeps, group.recvs = self.keeps + other.keeps, self.recvs + other.recvs
        group.stages = []
        for mine, others in zip(self.stages, other.stages):
            entries = {}
            for entry in mine + others:
                entries.setdefault(entry[:3] + entry[4:], []).extend(entry[3])
            if len(group.stages) == group.stage:
                group.stages.append(mine + others)
            else:
                group.stages.append([key[:3] + (tuple(names),) + key[3:] for key, names in entries.items()])
        return group

    def height(self, name):
        height, whole, _ = self.segments[name]
        slots, cut = self.state[name]
        return height if whole else height // cut * slots

    def start(self, sends):
        self.sends = sends
        self.recvs = [swap(send, *entry[:3]) for send, entry in zip(sends, self.stages[self.stage])]

    def begin(self, keep, send):
        entry = self.stages[0][len(self.keeps)]
        self.keeps.append(keep)
        self.recvs.append(swap(send, *entry[:3]))

    def fold(self):
        places = {}
        for source, entry in enumerate(self.stages[self.stage]):
            at = 0
            for name in entry[3]:
                places[name] = (source, at, self.height(name), self.state[name][0])
                at += self.height(name)
        shapes, moves, keeps, sends = [], [], [], []
        for entry in self.stages[self.stage + 1]:
            split = entry[4]
            keeps.append(len(shapes))
            sends.append(len(shapes) + (0 if split == "none" else 1))
            targets = (keeps[-1],) if split == "none" else (keeps[-1], sends[-1])
            to = 0
            for name in entry[3]:
                whole = self.segments[name][1]
                if split == "slots":
                    self.state[name][0] //= 2
                elif split == "rows":
                    self.state[name][1] = 2
                moves.append(places[name] + (targets, to, "none" if whole else split))
                to += self.height(name)
            shapes += [sds((to, TILE), BF16)] * len(targets)
        args = [x for pair in zip(self.keeps, self.recvs) for x in pair]
        out = call(functools.partial(fold_kernel, moves, len(args) // 2), args, shapes, 0.5, limit=4)
        self.keeps = [out[i] for i in keeps]
        self.sends = [out[i] for i in sends]
        self.stage += 1

    def left(self):
        return len(self.stages) - 1 - self.stage

    def pair(self):
        return self.keeps[0], self.recvs[0]


def result_kernel(sp_size, halved, *refs):
    outs = refs[8:16]
    gain_scr, shift_scr, qkv_scr, out_scr, up_scr, bup_scr, down_scr, bdown_scr = refs[16:24]
    mlp1, both, up0, qkv0 = refs[24:28]
    small_scr, sems = refs[28:]
    size = TILE // sp_size
    chunks = up_scr.shape[2] // TILE
    down_size = chunks * size
    row_half = lax.rem(lax.axis_index("grp"), 2)
    segments = (
        (mlp1, (chunks * size, down_size)), (both, (4 * size, down_size)),
        (up0, (chunks * size + size,)), (qkv0, (3 * size,)),
    )
    for i, (scr, heights) in enumerate(segments):
        mine, other = refs[2 * i], refs[2 * i + 1]
        at = 0
        base = 0
        for height in heights:
            if halved[i]:
                half = height // 2
                for ref, side in ((mine, row_half), (other, 1 - row_half)):
                    place = pl.ds(pl.multiple_of(base + side * half, 16), half)
                    scr[place, :] = ref[at : at + half, :].astype(F32)
                at += half
            else:
                span = slice(at, at + height)
                scr[base : base + height, :] = mine[span, :].astype(F32) + other[span, :].astype(F32)
                at += height
            base += height
    mine, other = refs[6], refs[7]
    at = 3 * size // (2 if halved[3] else 1)
    small = mine[at : at + 32, :].astype(F32)
    small_scr[...] = small if halved[3] else small + other[at : at + 32, :].astype(F32)
    for layer, (qkv, up, down, out, first, last) in enumerate((
        (qkv0, up0, both, up0, 4 * size, chunks * size),
        (both, mlp1, mlp1, both, chunks * size, 3 * size),
    )):
        for j in range(3):
            qkv_scr[layer, :, j * TILE : (j + 1) * TILE] = qkv[j * size : (j + 1) * size, :]
        for j in range(chunks):
            up_scr[layer, :, j * TILE : (j + 1) * TILE] = up[j * size : (j + 1) * size, :]
        down_scr[layer] = down[first : first + down_size, :]
        out_scr[layer] = out[last : last + size, :]
    sp = lax.axis_index("sp")
    back = lax.rem(TILE - sp * size, TILE)
    turned = pltpu.roll(small_scr[...], back, 1)
    for i in range(4):
        gain_scr[i : i + 1, :] = turned[8 * i : 8 * i + 1, :size]
        shift_scr[i : i + 1, :] = turned[8 * i + 1 : 8 * i + 2, :size]
    start = sp * down_size
    line = start // TILE
    back = lax.rem(TILE - lax.rem(start, TILE), TILE)
    for layer in range(2):
        first = 8 + 16 * layer
        bdown_scr[layer : layer + 1, :] = turned[first + 2 : first + 3, :size]
        rows = small_scr[first : first + 8, :]
        lines = lax.broadcasted_iota(jnp.int32, rows.shape, 0)
        picked = jnp.sum(jnp.where(lines == 4 + line, rows, 0.0), axis=0, keepdims=True)
        picked = pltpu.roll(jnp.broadcast_to(picked, rows.shape), back, 1)
        bup_scr[layer : layer + 1, :] = picked[0:1, :down_size]
    scrs = (gain_scr, shift_scr, qkv_scr, out_scr, up_scr, bup_scr, down_scr, bdown_scr)
    copies = [pltpu.make_async_copy(scr, out, sems.at[i]) for i, (scr, out) in enumerate(zip(scrs, outs))]
    for copy in copies:
        copy.start()
    for copy in copies:
        copy.wait()


VMEM = pl.BlockSpec(memory_space=pltpu.VMEM)
SMEM = pl.BlockSpec(memory_space=pltpu.SMEM)
HBM = pl.BlockSpec(memory_space=pltpu.HBM)


def sds(shape, dtype):
    return jax.ShapeDtypeStruct(shape, dtype)


def call(kernel, args, outs, micros, scratch=(), specs=None, out_specs=None, limit=12):
    return pl.pallas_call(
        kernel,
        in_specs=[VMEM] * len(args) if specs is None else specs,
        out_specs=[VMEM] * len(outs) if out_specs is None else out_specs,
        out_shape=outs,
        scratch_shapes=list(scratch),
        compiler_params=pltpu.CompilerParams(vmem_limit_bytes=limit * MIB),
        cost_estimate=pl.CostEstimate(flops=int(micros * COST), bytes_accessed=0, transcendentals=0),
    )(*args)


def swap(array, axis, size, bit):
    return lax.ppermute(array, axis, [(i, i ^ (1 << bit)) for i in range(size)])


def shards(sizes, tokens, frame_slot, norm_gain, norm_shift, w_qkv, w_out, w_up, b_up, w_down, b_down, cotangent):
    grp_size, sp_size = sizes
    frames, patches, width = tokens.shape
    hidden = w_up.shape[2]
    assert GROUP_FRAMES == 2 * frames and sp_size >= 8
    half = patches // 2
    rows = frames * patches
    sp_bits = sp_size.bit_length() - 1
    core_swap = functools.partial(swap, axis="sp", size=sp_size, bit=0)
    slots = sp_size // 2
    size = width // sp_size
    down_size = hidden // sp_size
    def slots_of(path):
        return [step for step in path if step != ROWS] + list(range(4, sp_bits))

    path_up1, path_down1 = (0, 1, 2, ROWS, 3), (0, 2, 1, ROWS, 3)
    path_attn1, path_down0 = (0, ROWS, 2, 1, 3), (0, 2, 1, ROWS, 3)
    path_up0, path_qkv0 = (0, 1, ROWS, 2, 3), (0, ROWS, 2, 1, 3)

    def row_out(cols, dtype=BF16):
        return sds((rows, cols), dtype)

    half_out = sds((frames, half, width), BF16)
    small_out = sds((8, TILE), F32)
    fence = lambda *arrays: lax.optimization_barrier(arrays)

    token = []

    def meet(groups, *arrays):
        recvs = [r for g in groups for r in g.recvs]
        out = list(fence(*arrays, *recvs, *token))
        count = len(arrays)
        arrays, recvs = out[:count], out[count:]
        for g in groups:
            g.recvs = [recvs.pop(0) for _ in g.recvs]
            g.fold()
        sends = [x for g in groups for x in g.sends]
        out = list(fence(*arrays, *sends))
        arrays, sends = out[:count], out[count:]
        for g in groups:
            g.start([sends.pop(0) for _ in g.sends])
        token[:] = [groups[-1].sends[-1]] if groups else []
        return arrays

    def buffers(height):
        return [sds((slots * height, TILE), BF16)] * 2

    cot_recv = core_swap(cotangent)
    widen = lambda a: jnp.pad(a, ((0, 0), (0, hidden - width)))
    packed = jnp.concatenate([widen(norm_gain), widen(norm_shift), b_up, widen(b_down)], axis=0)
    weights = (w_qkv, w_out, w_up, w_down)
    shapes = [sds(w.shape[1:], BF16) for w in weights]
    out = call(
        space_forward_kernel,
        (tokens, packed) + weights,
        [
            half_out, half_out, row_out(width), row_out(3 * width), sds((frames, HEADS, patches), F32),
            row_out(width), row_out(width, F32), row_out(width), row_out(hidden), row_out(hidden),
        ],
        16,
        scratch=[pltpu.VMEM(tokens.shape, BF16)]
        + [pltpu.VMEM(x.shape, BF16) for x in shapes]
        + [
            pltpu.VMEM((2, patches, width), BF16), pltpu.VMEM((2, patches, 3 * width), BF16),
            pltpu.VMEM((2, patches, width), BF16), pltpu.VMEM((2, patches, width), F32),
            pltpu.VMEM((2, patches, width), BF16),
            pltpu.VMEM((2, patches, hidden), BF16), pltpu.VMEM((2, patches, hidden), BF16),
            pltpu.VMEM((patches, width), F32), pltpu.SemaphoreType.DMA((5,)),
            pltpu.SemaphoreType.DMA((14,)),
        ],
        specs=[HBM, VMEM] + [HBM] * 4,
        out_specs=[VMEM, VMEM, HBM, HBM, VMEM] + [HBM] * 5,
        limit=LIMIT1,
    )
    (x_keep, x_send, h0, qkv0, lse0, o0, xa, h1, act0, slope0) = out
    x_recv = core_swap(x_send)

    place_scratch = [
        pltpu.SMEM((GROUP_FRAMES,), jnp.int32),
        pltpu.VMEM((GROUP_FRAMES, half, width), BF16),
    ]
    (out_own, out_send, xt, h2, qkv1, o1, h3, act1, du1, gr1, dxb, small3, w_qkv1, w_out1) = call(
        time_forward_kernel,
        (frame_slot, x_keep, x_recv, cotangent, cot_recv, packed) + weights,
        [
            half_out, half_out, row_out(width), row_out(width), row_out(3 * width), row_out(width),
            row_out(width), row_out(hidden), row_out(hidden), row_out(width), row_out(width, F32),
            small_out,
        ] + shapes[:2],
        24,
        scratch=place_scratch
        + [pltpu.VMEM((rows // 4, hidden), BF16)]
        + [pltpu.VMEM(x.shape, BF16) for x in shapes[2:]]
        + [pltpu.SemaphoreType.DMA((4,))],
        specs=[SMEM] + [VMEM] * 5 + [HBM] * 4,
        limit=LIMIT2,
    )
    out_recv = core_swap(out_send)

    out = call(
        functools.partial(mlp_weights_kernel, (slots_of(path_up1), slots_of(path_down1))), (h3, du1, act1, gr1),
        buffers(4 * size + down_size), 4.5,
    )
    keep, send, dxb = fence(*out, dxb)
    mlp1 = Group(sizes, {"up": (4 * size, False, path_up1), "down": (down_size, False, path_down1)})
    mlp1.begin(keep, send)

    (dx_own, dx_send, ar1, dqkv1, small2) = call(
        time_backward_kernel,
        (frame_slot, xt, qkv1, dxb, packed, w_qkv1, w_out1),
        [half_out, half_out, row_out(width), row_out(3 * width), small_out],
        8,
        scratch=place_scratch,
        specs=[SMEM] + [VMEM] * 6,
    )
    dx_recv = core_swap(dx_send)
    keep, send = call(
        functools.partial(attn_weights_kernel, slots_of(path_attn1)), (h2, dqkv1, o1, ar1),
        buffers(4 * size), 2.4,
    )
    dx_own, dx_recv, keep, send, out_recv = meet((mlp1,), dx_own, dx_recv, keep, send, out_recv)
    attn1 = Group(sizes, {"attn": (4 * size, False, path_attn1)})
    attn1.begin(keep, send)
    gr0, keep_down, send_down = call(
        functools.partial(down_weights_kernel, slots_of(path_down0)), (act0, dx_own, dx_recv),
        [row_out(width)] + buffers(down_size), 2.4,
    )
    (du0, dxa, ar0, small1) = call(
        space_mlp_back_kernel,
        (gr0, xa, slope0, packed, w_up, w_down),
        [row_out(hidden), row_out(width, F32), row_out(width), small_out],
        6,
    )
    keep_up, send_up = call(
        functools.partial(up_weights_kernel, slots_of(path_up0)), (h1, du0, o0, ar0), buffers(5 * size), 3
    )
    keep_down, send_down, keep_up, send_up, ar0 = meet(
        (mlp1, attn1), keep_down, send_down, keep_up, send_up, ar0
    )
    down0 = Group(sizes, {"down": (down_size, False, path_down0)})
    down0.begin(keep_down, send_down)
    up0 = Group(sizes, {"up": (5 * size, False, path_up0)})
    up0.begin(keep_up, send_up)

    (dqkv0,) = call(
        space_attn_back_kernel, (ar0, qkv0, lse0, o0, w_out), [row_out(3 * width)], 10
    )
    keep, send = call(
        functools.partial(qkv_weights_kernel, slots_of(path_qkv0)), (dqkv0, h0), buffers(3 * size), 2
    )
    dqkv0, keep, send, *attn1.recvs = meet((up0, down0, mlp1), dqkv0, keep, send, *attn1.recvs)
    both = attn1.beside(down0)
    qkv = Group(
        sizes, {"qkv": (3 * size, False, path_qkv0), "small": (32, True, path_qkv0)}, apart=True
    )
    qkv.begin(keep, send)
    grad_tokens, output, small = call(
        finish_kernel,
        (
            dqkv0, tokens, dxa, out_own, out_recv, packed, w_qkv, small1, small2, small3,
        ),
        [sds(tokens.shape, BF16), sds(tokens.shape, BF16), sds((32, TILE), BF16)],
        4,
        scratch=[pltpu.VMEM((8, TILE), F32)],
    )
    (small,) = fence(small)
    qkv.begin(small, small)
    everyone = (mlp1, both, up0, qkv)
    for names in TAIL:
        groups = [g for g in (dict(zip("mbuq", everyone))[c] for c in names) if g.left()]
        if groups:
            meet(groups)
    while any(g.left() for g in everyone):
        meet([g for g in everyone if g.left()])
    finals = [
        sds((4, size), F32), sds((4, size), F32), sds((2, size, 3 * width), F32), sds((2, size, width), F32),
        sds((2, size, hidden), F32), sds((2, down_size), F32), sds((2, down_size, width), F32),
        sds((2, size), F32),
    ]
    heights = (4 * size + down_size, 4 * size + down_size, 5 * size, 3 * size)
    results = call(
        functools.partial(result_kernel, sp_size, tuple(g.halved for g in everyone)),
        [x for g in everyone for x in g.pair()], finals, 2,
        scratch=[pltpu.VMEM(f.shape, F32) for f in finals]
        + [pltpu.VMEM((h, TILE), F32) for h in heights]
        + [pltpu.VMEM((32, TILE), F32), pltpu.SemaphoreType.DMA((8,))],
        out_specs=[HBM] * 8,
    )
    return (output, grad_tokens, *results)


def solution(mesh):
    rows = P(("grp", "sp"), None, None)
    in_specs = (rows, P("grp", None), P(), P(), P(), P(), P(), P(), P(), P(), rows)
    out_specs = (
        rows, rows, P(None, "sp"), P(None, "sp"), P(None, "sp", None), P(None, "sp", None),
        P(None, "sp", None), P(None, "sp"), P(None, "sp", None), P(None, "sp"),
    )
    body = functools.partial(shards, (mesh.shape["grp"], mesh.shape["sp"]))
    return jax.shard_map(body, mesh=mesh, in_specs=in_specs, out_specs=out_specs, check_vma=False)
```

profile of v0, /device:TPU:0, one launch (start us, length us, event | category | flops | bytes accessed | tf_op | source)
XLA Modules:
  0.0 155.8 jit_solution(14792727992979377218)
XLA Ops:
  0.6 0.5 collective-permute-start.1
  1.2 0.8 select_maximum_fusion.params_ref
  2.0 20.9 %shard_map.186 = (bf16[4,128,512]{2,1,0:T(8,128)(2,1)S(1)}, bf16[4,128,512]{2,1,0:T(8,128)(2,1)S(1)}, bf16[1024,512]{1,0:T(8,128)(2,1)}, bf16[1024,1536]{1,0:T(8...) custom-call(bf16[4,256,512]{2,1,0:T(8,128)(2,1)} %tok_ref.1, ...), custom_call_target="tpu_custom_call" | custom-call | flops 368000000 | tf_op jit(solution)/shard_map/pallas_call | solution.py:854
  23.0 1.9 %collective-permute-done.recv_ref = bf16[4,128,512]{2,1,0:T(8,128)(2,1)S(1)} collective-permute-done((bf16[4,128,512]{2,1,0:T(8,128)(2,1)S(1)}, bf16[4,128,512]{2,1,0:T(8,128)(2,1)S(1)}, u32[]{:S(2)}, u32[]{:S(2)}) %collective-permute-start) | collective-permute-done | bytes 524320 | tf_op jit(solution)/shard_map/ppermute | solution.py:866
  24.9 21.2 %shard_map.187 = (bf16[4,128,512]{2,1,0:T(8,128)(2,1)S(1)}, bf16[4,128,512]{2,1,0:T(8,128)(2,1)S(1)}, bf16[1024,512]{1,0:T(8,128)(2,1)S(1)}, bf16[1024,512]{1,0:...) custom-call(s32[8,8]{1,0:T(8,128)S(1)} %copy-done.13, ...), custom_call_target="tpu_custom_call" | custom-call | flops 552000000 | tf_op jit(solution)/shard_map/pallas_call | solution.py:854
  46.0 4.6 %shard_map.188 = (bf16[2048,512]{1,0:T(8,128)(2,1)S(1)}, bf16[2048,512]{1,0:T(8,128)(2,1)S(1)}) custom-call(bf16[1024,512]{1,0:T(8,128)(2,1)S(1)} %get-tuple-element.188.h_ref, bf16[1024,2048]{1,0:T(8,128)(2,1)S(1)} %get-tuple-element.189.du_ref, bf16[1024,2048]{1,0:T(8,128)(2,1)S(1)} %get-tuple-element.190.act_ref, ...), custom_call_target="tpu_custom_call" | custom-call | flops 103500000 | tf_op jit(solution)/shard_map/pallas_call | solution.py:854
  51.2 8.0 %shard_map.189 = (bf16[4,128,512]{2,1,0:T(8,128)(2,1)S(1)}, bf16[4,128,512]{2,1,0:T(8,128)(2,1)S(1)}, bf16[1024,512]{1,0:T(8,128)(2,1)S(1)}, bf16[1024,1536]{1,0:T(8,128)(2,1)S(1)}, f32[8,512]{1,0:T(8,128)S(1)}) custom-call(s32[8,8]{1,0:T(8,128)S(1)} %copy-done.13, bf16[1024,512]{1,0:T(8,128)(2,1)S(1)} %get-tuple-element.186.x_ref, ...), custom_call_target="tpu_custom_call" | custom-call | flops 184000000 | tf_op jit(solution)/shard_map/pallas_call | solution.py:854
  59.4 2.4 %shard_map.190 = (bf16[1024,512]{1,0:T(8,128)(2,1)S(1)}, bf16[1024,512]{1,0:T(8,128)(2,1)S(1)}) custom-call(bf16[1024,512]{1,0:T(8,128)(2,1)S(1)} %get-tuple-element.200.h_ref, bf16[1024,1536]{1,0:T(8,128)(2,1)S(1)} %get-tuple-element.201.dqkv_ref, bf16[1024,512]{1,0:T(8,128)(2,1)S(1)} %get-tuple-element.202.o_ref, ...), custom_call_target="tpu_custom_call" | custom-call | flops 55200000 | tf_op jit(solution)/shard_map/pallas_call | solution.py:854
  62.6 2.6 %collective-permute-start.5 = (bf16[512,512]{1,0:T(8,128)(2,1)S(1)}, bf16[512,512]{1,0:T(8,128)(2,1)S(1)}, u32[]{:S(2)}, u32[]{:S(2)}) collective-permute-start(bf16[512,512]{1,0:T(8,128)(2,1)S(1)} %get-tuple-element.230), channel_id=1, source_target_pairs={{0,2},{1,3},{2,0},{3,1},{4,6},{5,7},{6,4},{7,5},{8,10},{9,11},{10,... | collective-permute-start | bytes 1572872 | tf_op jit(solution)/shard_map/ppermute | solution.py:866
  65.2 1.6 collective-permute-start.6
  66.8 2.4 %shard_map.192 = (bf16[1024,512]{1,0:T(8,128)(2,1)S(1)}, bf16[1024,512]{1,0:T(8,128)(2,1)S(1)}, bf16[1024,512]{1,0:T(8,128)(2,1)S(1)}) custom-call(bf16[1024,2048]{1,0:T(8,128)(2,1)S(1)} %copy-done.5, bf16[4,128,512]{2,1,0:T(8,128)(2,1)S(1)} %get-tuple-element.217.own_ref, bf16[4,128,512]{2,1,0:T(8,128)(2,1)S(1)} %collective-permute-done.2.recv_ref), custom_call_target="tpu_custom_call" | custom-call | flops 55200000 | tf_op jit(solution)/shard_map/pallas_call | solution.py:854
  69.3 6.6 %shard_map.193 = (bf16[1024,2048]{1,0:T(8,128)(2,1)S(1)}, f32[1024,512]{1,0:T(8,128)S(1)}, bf16[1024,512]{1,0:T(8,128)(2,1)S(1)}, f32[8,512]{1,0:T(8,128)S(1)}) custom-call(bf16[1024,512]{1,0:T(8,128)(2,1)S(1)} %get-tuple-element.222.gr_ref, f32[1024,512]{1,0:T(8,128)S(1)} %copy-done.9, bf16[1024,2048]{1,0:T(8,128)(2,1)S(1)} %copy-done.6, ...), custom_call_target="tpu_custom_call" | custom-call | flops 138000000 | tf_op jit(solution)/shard_map/pallas_call | solution.py:854
  75.9 2.9 %shard_map.194 = (bf16[1280,512]{1,0:T(8,128)(2,1)S(1)}, bf16[1280,512]{1,0:T(8,128)(2,1)S(1)}) custom-call(bf16[1024,512]{1,0:T(8,128)(2,1)S(1)} %copy-done.11, bf16[1024,2048]{1,0:T(8,128)(2,1)S(1)} %get-tuple-element.225.du_ref, bf16[1024,512]{1,0:T(8,128)(2,1)S(1)} %copy-done.4, bf16[1024,512]{1,0:T(8,128)(2,1)S(1)} %get-tuple-element.247.ar_ref), custom_call_target="tpu_custom_call" | custom-call | flops 69000000 | tf_op jit(solution)/shard_map/pallas_call | solution.py:854
  79.5 0.5 collective-permute-start.10
  80.0 1.5 collective-permute-start.8
  81.5 1.6 %collective-permute-start.11 = (bf16[256,512]{1,0:T(8,128)(2,1)S(1)}, bf16[256,512]{1,0:T(8,128)(2,1)S(1)}, u32[]{:S(2)}, u32[]{:S(2)}) collective-permute-start(bf16[256,512]{1,0:T(8,128)(2,1)S(1)} %get-tuple-element.256), channel_id=1, source_target_pairs={{0,4},{1,5},{2,6},{3,7},{4,0},{5,1},{6,2},{7,3},{8,12},{9,13},{10,... | collective-permute-start | bytes 786440 | tf_op jit(solution)/shard_map/ppermute | solution.py:866
  83.1 0.5 collective-permute-start.12
  83.6 10.7 %shard_map.197.dqkv_ref = bf16[1024,1536]{1,0:T(8,128)(2,1)S(1)} custom-call(bf16[1024,512]{1,0:T(8,128)(2,1)S(1)} %get-tuple-element.247.ar_ref, bf16[1024,1536]{1,0:T(8,128)(2,1)S(1)} %copy-done.8, f32[4,8,256]{2,1,0:T(8,128)S(1)} %get-tuple-element.249.lse_ref, bf16[1024,512]{1,0:T(8,128)(2,1)S(1)} %copy-done.4, bf16[2,512,512]{2,1,0:T(8,128)(2,1)S(1)} %copy-done.3), custom_call_target="tpu_custom_call" | custom-call | flops 230000000 | tf_op jit(solution)/shard_map/pallas_call | solution.py:854
  94.3 1.8 %shard_map.198 = (bf16[768,512]{1,0:T(8,128)(2,1)S(1)}, bf16[768,512]{1,0:T(8,128)(2,1)S(1)}) custom-call(bf16[1024,1536]{1,0:T(8,128)(2,1)S(1)} %shard_map.197.dqkv_ref, bf16[1024,512]{1,0:T(8,128)(2,1)S(1)} %copy-done.12), custom_call_target="tpu_custom_call" | custom-call | flops 46000000 | tf_op jit(solution)/shard_map/pallas_call | solution.py:854
  96.7 1.6 %collective-permute-start.19 = (bf16[640,512]{1,0:T(8,128)(2,1)S(1)}, bf16[640,512]{1,0:T(8,128)(2,1)S(1)}, u32[]{:S(2)}, u32[]{:S(2)}) collective-permute-start(bf16[640,512]{1,0:T(8,128)(2,1)S(1)} %get-tuple-element.297), channel_id=1, source_target_pairs={{0,2},{1,3},{2,0},{3,1},{4,6},{5,7},{6,4},{7,5},{8,10},{9,11},{10,... | collective-permute-start | bytes 1966088 | tf_op jit(solution)/shard_map/ppermute | solution.py:866
  98.3 0.5 collective-permute-start.18
  98.7 0.5 collective-permute-start.13
  99.2 4.4 %shard_map.202 = (bf16[4,256,512]{2,1,0:T(8,128)(2,1)}, bf16[4,256,512]{2,1,0:T(8,128)(2,1)}, bf16[32,512]{1,0:T(8,128)(2,1)S(1)}) custom-call(bf16[1024,1536]{1,0:T(8,128)(2,1)S(1)} %shard_map.197.dqkv_ref, bf16[4,256,512]{2,1,0:T(8,128)(2,1)S(1)} %copy-done.7, f32[1024,512]{1,0:T(8,128)S(1)} %get-tuple-element.274.dxa_ref, ...), custom_call_target="tpu_custom_call" | custom-call | flops 92000000 | tf_op jit(solution)/shard_map/pallas_call | solution.py:854
  103.6 1.2 collective-permute-done.15.refs_3_
  104.9 1.6 %collective-permute-start.17 = (bf16[416,512]{1,0:T(8,128)(2,1)S(1)}, bf16[416,512]{1,0:T(8,128)(2,1)S(1)}, u32[]{:S(2)}, u32[]{:S(2)}) collective-permute-start(bf16[416,512]{1,0:T(8,128)(2,1)S(1)} %get-tuple-element.289), channel_id=1, source_target_pairs={{0,16},{16,0},{1,17},{17,1},{2,18},{18,2},{3,19},{19,3},{4,20},{20... | collective-permute-start | bytes 1277960 | tf_op jit(solution)/shard_map/ppermute | solution.py:866
  106.9 5.4 %collective-permute-done.18.refs_3_ = bf16[512,512]{1,0:T(8,128)(2,1)S(1)} collective-permute-done((bf16[512,512]{1,0:T(8,128)(2,1)S(1)}, bf16[512,512]{1,0:T(8,128)(2,1)S(1)}, u32[]{:S(2)}, u32[]{:S(2)}) %collective-permute-start.18) | collective-permute-done | bytes 524320 | tf_op jit(solution)/shard_map/ppermute | solution.py:866
  112.3 1.6 %collective-permute-done.19.refs_1_ = bf16[640,512]{1,0:T(8,128)(2,1)S(1)} collective-permute-done((bf16[640,512]{1,0:T(8,128)(2,1)S(1)}, bf16[640,512]{1,0:T(8,128)(2,1)S(1)}, u32[]{:S(2)}, u32[]{:S(2)}) %collective-permute-start.19) | collective-permute-done | bytes 655392 | tf_op jit(solution)/shard_map/ppermute | solution.py:866
  114.0 0.6 collective-permute-start.23
  114.9 1.7 %collective-permute-start.22 = (bf16[256,512]{1,0:T(8,128)(2,1)S(1)}, bf16[256,512]{1,0:T(8,128)(2,1)S(1)}, u32[]{:S(2)}, u32[]{:S(2)}) collective-permute-start(bf16[256,512]{1,0:T(8,128)(2,1)S(1)} %get-tuple-element.312), channel_id=1, source_target_pairs={{0,2},{1,3},{2,0},{3,1},{4,6},{5,7},{6,4},{7,5},{8,10},{9,11},{10,... | collective-permute-start | bytes 786440 | tf_op jit(solution)/shard_map/ppermute | solution.py:866
  116.6 2.6 %collective-permute-start.16 = (bf16[128,512]{1,0:T(8,128)(2,1)S(1)}, bf16[128,512]{1,0:T(8,128)(2,1)S(1)}, u32[]{:S(2)}, u32[]{:S(2)}) collective-permute-start(bf16[128,512]{1,0:T(8,128)(2,1)S(1)} %get-tuple-element.292), channel_id=1, source_target_pairs={{0,8},{1,9},{2,10},{3,11},{4,12},{5,13},{6,14},{7,15},{8,0},{9,1},... | collective-permute-start | bytes 393224 | tf_op jit(solution)/shard_map/ppermute | solution.py:866
  119.2 1.7 %collective-permute-start.27 = (bf16[224,512]{1,0:T(8,128)(2,1)S(1)}, bf16[224,512]{1,0:T(8,128)(2,1)S(1)}, u32[]{:S(2)}, u32[]{:S(2)}) collective-permute-start(bf16[224,512]{1,0:T(8,128)(2,1)S(1)} %get-tuple-element.308), channel_id=1, source_target_pairs={{0,4},{1,5},{2,6},{3,7},{4,0},{5,1},{6,2},{7,3},{8,12},{9,13},{10,... | collective-permute-start | bytes 688136 | tf_op jit(solution)/shard_map/ppermute | solution.py:866
  120.9 3.6 %collective-permute-done.16.refs_1_ = bf16[128,512]{1,0:T(8,128)(2,1)S(1)} collective-permute-done((bf16[128,512]{1,0:T(8,128)(2,1)S(1)}, bf16[128,512]{1,0:T(8,128)(2,1)S(1)}, u32[]{:S(2)}, u32[]{:S(2)}) %collective-permute-start.16) | collective-permute-done | bytes 131104 | tf_op jit(solution)/shard_map/ppermute | solution.py:866
  124.5 2.2 %collective-permute-done.21.refs_1_ = bf16[256,512]{1,0:T(8,128)(2,1)S(1)} collective-permute-done((bf16[256,512]{1,0:T(8,128)(2,1)S(1)}, bf16[256,512]{1,0:T(8,128)(2,1)S(1)}, u32[]{:S(2)}, u32[]{:S(2)}) %collective-permute-start.21) | collective-permute-done | bytes 262176 | tf_op jit(solution)/shard_map/ppermute | solution.py:866
  126.8 2.7 %collective-permute-start.26 = (bf16[160,512]{1,0:T(8,128)(2,1)S(1)}, bf16[160,512]{1,0:T(8,128)(2,1)S(1)}, u32[]{:S(2)}, u32[]{:S(2)}) collective-permute-start(bf16[160,512]{1,0:T(8,128)(2,1)S(1)} %get-tuple-element.324), channel_id=1, source_target_pairs={{0,4},{1,5},{2,6},{3,7},{4,0},{5,1},{6,2},{7,3},{8,12},{9,13},{10,... | collective-permute-start | bytes 491528 | tf_op jit(solution)/shard_map/ppermute | solution.py:866
  129.5 1.5 collective-permute-start.24
  131.0 1.5 collective-permute-start.25
  132.5 0.6 collective-permute-start.30
  133.1 1.3 collective-permute-done.24.refs_1_
  134.5 1.5 collective-permute-done.25.refs_3_
  136.5 2.5 %collective-permute-start.29 = (bf16[80,512]{1,0:T(8,128)(2,1)S(1)}, bf16[80,512]{1,0:T(8,128)(2,1)S(1)}, u32[]{:S(2)}, u32[]{:S(2)}) collective-permute-start(bf16[80,512]{1,0:T(8,128)(2,1)S(1)} %get-tuple-element.337), channel_id=1, source_target_pairs={{0,8},{1,9},{2,10},{3,11},{4,12},{5,13},{6,14},{7,15},{8,0},{9,1},... | collective-permute-start | bytes 245768 | tf_op jit(solution)/shard_map/ppermute | solution.py:866
  139.5 1.5 collective-permute-start.20
  141.0 6.2 %collective-permute-done.29.refs_1_ = bf16[80,512]{1,0:T(8,128)(2,1)S(1)} collective-permute-done((bf16[80,512]{1,0:T(8,128)(2,1)S(1)}, bf16[80,512]{1,0:T(8,128)(2,1)S(1)}, u32[]{:S(2)}, u32[]{:S(2)}) %collective-permute-start.29) | collective-permute-done | bytes 81952 | tf_op jit(solution)/shard_map/ppermute | solution.py:866
  147.3 1.6 %collective-permute-start.31 = (bf16[128,512]{1,0:T(8,128)(2,1)S(1)}, bf16[128,512]{1,0:T(8,128)(2,1)S(1)}, u32[]{:S(2)}, u32[]{:S(2)}) collective-permute-start(bf16[128,512]{1,0:T(8,128)(2,1)S(1)} %shard_map.215.refs_2_), channel_id=1, source_target_pairs={{0,16},{16,0},{1,17},{17,1},{2,18},{18,2},{3,19},{19,3},{4,20},{20... | collective-permute-start | bytes 393224 | tf_op jit(solution)/shard_map/ppermute | solution.py:866
  148.9 0.5 collective-permute-start.32
  149.4 1.6 %collective-permute-start.34 = (bf16[80,512]{1,0:T(8,128)(2,1)S(1)}, bf16[80,512]{1,0:T(8,128)(2,1)S(1)}, u32[]{:S(2)}, u32[]{:S(2)}) collective-permute-start(bf16[80,512]{1,0:T(8,128)(2,1)S(1)} %shard_map.217.refs_6_), channel_id=1, source_target_pairs={{0,16},{16,0},{1,17},{17,1},{2,18},{18,2},{3,19},{19,3},{4,20},{20... | collective-permute-start | bytes 245768 | tf_op jit(solution)/shard_map/ppermute | solution.py:866
  151.0 2.3 %collective-permute-done.32.refs_5_ = bf16[80,512]{1,0:T(8,128)(2,1)S(1)} collective-permute-done((bf16[80,512]{1,0:T(8,128)(2,1)S(1)}, bf16[80,512]{1,0:T(8,128)(2,1)S(1)}, u32[]{:S(2)}, u32[]{:S(2)}) %collective-permute-start.32) | collective-permute-done | bytes 81952 | tf_op jit(solution)/shard_map/ppermute | solution.py:866
  153.3 0.9 collective-permute-done.34.refs_7_
  154.2 1.4 shard_map.218
  (84 shorter events, 4.9 us)
Async XLA Ops:
  0.6 24.2 %collective-permute-start.1 = (bf16[4,256,512]{2,1,0:T(8,128)(2,1)}, bf16[4,256,512]{2,1,0:T(8,128)(2,1)S(1)}, u32[]{:S(2)}, u32[]{:S(2)}) collective-permute-start(bf16[4,256,512]{2,1,0:T(8,128)(2,1)} %cot_ref.1), channel_id=1, source_target_pairs={{0,1},{1,0},{2,3},{3,2},{4,5},{5,4},{6,7},{7,6},{8,9},{9,8},{10,11... | collective-permute-start | bytes 3145736 | tf_op jit(solution)/shard_map/ppermute | solution.py:866
  1.9 22.9 %copy-start.2 = (bf16[2,512,1536]{2,1,0:T(8,128)(2,1)S(1)}, bf16[2,512,1536]{2,1,0:T(8,128)(2,1)}, u32[]{:S(2)}) copy-start(bf16[2,512,1536]{2,1,0:T(8,128)(2,1)} %wqkv_ref.1) | copy-start | bytes 9437188
  2.0 22.9 %copy-start.3 = (bf16[2,512,512]{2,1,0:T(8,128)(2,1)S(1)}, bf16[2,512,512]{2,1,0:T(8,128)(2,1)}, u32[]{:S(2)}) copy-start(bf16[2,512,512]{2,1,0:T(8,128)(2,1)} %wout_ref.1) | copy-start | bytes 3145732
  2.0 22.9 %copy-start.10 = (bf16[4,256,512]{2,1,0:T(8,128)(2,1)S(1)}, bf16[4,256,512]{2,1,0:T(8,128)(2,1)}, u32[]{:S(2)}) copy-start(bf16[4,256,512]{2,1,0:T(8,128)(2,1)} %cot_ref.1) | copy-start | bytes 3145732
  2.0 22.9 %copy-start.13 = (s32[8,8]{1,0:T(8,128)S(1)}, s32[8,8]{1,0:T(8,128)}, u32[]{:S(2)}) copy-start(s32[8,8]{1,0:T(8,128)} %slots_ref.3) | copy-start | bytes 772
  22.9 2.0 %collective-permute-start = (bf16[4,128,512]{2,1,0:T(8,128)(2,1)S(1)}, bf16[4,128,512]{2,1,0:T(8,128)(2,1)S(1)}, u32[]{:S(2)}, u32[]{:S(2)}) collective-permute-start(bf16[4,128,512]{2,1,0:T(8,128)(2,1)S(1)} %get-tuple-element.185), channel_id=1, source_target_pairs={{0,1},{1,0},{2,3},{3,2},{4,5},{5,4},{6,7},{7,6},{8,9},{9,8},{10,11... | collective-permute-start | bytes 1572872 | tf_op jit(solution)/shard_map/ppermute | solution.py:866
  50.6 11.2 %collective-permute-start.4 = (bf16[2048,512]{1,0:T(8,128)(2,1)S(1)}, bf16[2048,512]{1,0:T(8,128)(2,1)S(1)}, u32[]{:S(2)}, u32[]{:S(2)}) collective-permute-start(bf16[2048,512]{1,0:T(8,128)(2,1)S(1)} %get-tuple-element.207), channel_id=1, source_target_pairs={{0,1},{1,0},{2,3},{3,2},{4,5},{5,4},{6,7},{7,6},{8,9},{9,8},{10,11... | collective-permute-start | bytes 6291464 | tf_op jit(solution)/shard_map/ppermute | solution.py:866
  50.8 11.0 %collective-permute-start.3 = (bf16[4,128,512]{2,1,0:T(8,128)(2,1)S(1)}, bf16[4,128,512]{2,1,0:T(8,128)(2,1)S(1)}, u32[]{:S(2)}, u32[]{:S(2)}) collective-permute-start(bf16[4,128,512]{2,1,0:T(8,128)(2,1)S(1)} %get-tuple-element.206), channel_id=1, source_target_pairs={{0,1},{1,0},{2,3},{3,2},{4,5},{5,4},{6,7},{7,6},{8,9},{9,8},{10,11... | collective-permute-start | bytes 1572872 | tf_op jit(solution)/shard_map/ppermute | solution.py:866
  51.2 18.0 %copy-start.6 = (bf16[1024,2048]{1,0:T(8,128)(2,1)S(1)}, bf16[1024,2048]{1,0:T(8,128)(2,1)}, u32[]{:S(2)}) copy-start(bf16[1024,2048]{1,0:T(8,128)(2,1)} %get-tuple-element.224.slope_ref) | copy-start | bytes 12582916
  59.2 2.6 %collective-permute-start.2 = (bf16[4,128,512]{2,1,0:T(8,128)(2,1)S(1)}, bf16[4,128,512]{2,1,0:T(8,128)(2,1)S(1)}, u32[]{:S(2)}, u32[]{:S(2)}) collective-permute-start(bf16[4,128,512]{2,1,0:T(8,128)(2,1)S(1)} %get-tuple-element.199), channel_id=1, source_target_pairs={{0,1},{1,0},{2,3},{3,2},{4,5},{5,4},{6,7},{7,6},{8,9},{9,8},{10,11... | collective-permute-start | bytes 1572872 | tf_op jit(solution)/shard_map/ppermute | solution.py:866
  59.4 7.4 %copy-start.5 = (bf16[1024,2048]{1,0:T(8,128)(2,1)S(1)}, bf16[1024,2048]{1,0:T(8,128)(2,1)}, u32[]{:S(2)}) copy-start(bf16[1024,2048]{1,0:T(8,128)(2,1)} %get-tuple-element.183.act_ref) | copy-start | bytes 12582916
  59.4 9.8 %copy-start.9 = (f32[1024,512]{1,0:T(8,128)S(1)}, f32[1024,512]{1,0:T(8,128)}, u32[]{:S(2)}) copy-start(f32[1024,512]{1,0:T(8,128)} %get-tuple-element.223.xa_ref) | copy-start | bytes 6291460
  61.8 7.4 %copy-start.1 = (bf16[2,2048,512]{2,1,0:T(8,128)(2,1)S(1)}, bf16[2,2048,512]{2,1,0:T(8,128)(2,1)}, u32[]{:S(2)}) copy-start(bf16[2,2048,512]{2,1,0:T(8,128)(2,1)} %wdown_ref.1) | copy-start | bytes 12582916
  62.2 7.1 %copy-start = (bf16[2,512,2048]{2,1,0:T(8,128)(2,1)S(1)}, bf16[2,512,2048]{2,1,0:T(8,128)(2,1)}, u32[]{:S(2)}) copy-start(bf16[2,512,2048]{2,1,0:T(8,128)(2,1)} %wup_ref.1) | copy-start | bytes 12582916
  62.2 17.0 %collective-permute-start.7 = (bf16[1024,512]{1,0:T(8,128)(2,1)S(1)}, bf16[1024,512]{1,0:T(8,128)(2,1)S(1)}, u32[]{:S(2)}, u32[]{:S(2)}) collective-permute-start(bf16[1024,512]{1,0:T(8,128)(2,1)S(1)} %get-tuple-element.232), channel_id=1, source_target_pairs={{0,1},{1,0},{2,3},{3,2},{4,5},{5,4},{6,7},{7,6},{8,9},{9,8},{10,11... | collective-permute-start | bytes 3145736 | tf_op jit(solution)/shard_map/ppermute | solution.py:866
  62.6 16.2 %collective-permute-start.5 = (bf16[512,512]{1,0:T(8,128)(2,1)S(1)}, bf16[512,512]{1,0:T(8,128)(2,1)S(1)}, u32[]{:S(2)}, u32[]{:S(2)}) collective-permute-start(bf16[512,512]{1,0:T(8,128)(2,1)S(1)} %get-tuple-element.230), channel_id=1, source_target_pairs={{0,2},{1,3},{2,0},{3,1},{4,6},{5,7},{6,4},{7,5},{8,10},{9,11},{10,... | collective-permute-start | bytes 1572872 | tf_op jit(solution)/shard_map/ppermute | solution.py:866
  65.2 13.9 %collective-permute-start.6 = (bf16[512,512]{1,0:T(8,128)(2,1)S(1)}, bf16[512,512]{1,0:T(8,128)(2,1)S(1)}, u32[]{:S(2)}, u32[]{:S(2)}) collective-permute-start(bf16[512,512]{1,0:T(8,128)(2,1)S(1)} %get-tuple-element.231), channel_id=1, source_target_pairs={{0,4},{1,5},{2,6},{3,7},{4,0},{5,1},{6,2},{7,3},{8,12},{9,13},{10,... | collective-permute-start | bytes 1572872 | tf_op jit(solution)/shard_map/ppermute | solution.py:866
  69.3 6.6 %copy-start.4 = (bf16[1024,512]{1,0:T(8,128)(2,1)S(1)}, bf16[1024,512]{1,0:T(8,128)(2,1)}, u32[]{:S(2)}) copy-start(bf16[1024,512]{1,0:T(8,128)(2,1)} %get-tuple-element.226.o_ref) | copy-start | bytes 3145732
  69.3 6.6 %copy-start.11 = (bf16[1024,512]{1,0:T(8,128)(2,1)S(1)}, bf16[1024,512]{1,0:T(8,128)(2,1)}, u32[]{:S(2)}) copy-start(bf16[1024,512]{1,0:T(8,128)(2,1)} %get-tuple-element.221.h_ref) | copy-start | bytes 3145732
  78.8 4.8 %copy-start.8 = (bf16[1024,1536]{1,0:T(8,128)(2,1)S(1)}, bf16[1024,1536]{1,0:T(8,128)(2,1)}, u32[]{:S(2)}) copy-start(bf16[1024,1536]{1,0:T(8,128)(2,1)} %get-tuple-element.248.qkv_ref) | copy-start | bytes 9437188
  79.4 16.8 %collective-permute-start.9 = (bf16[1280,512]{1,0:T(8,128)(2,1)S(1)}, bf16[1280,512]{1,0:T(8,128)(2,1)S(1)}, u32[]{:S(2)}, u32[]{:S(2)}) collective-permute-start(bf16[1280,512]{1,0:T(8,128)(2,1)S(1)} %get-tuple-element.254), channel_id=1, source_target_pairs={{0,1},{1,0},{2,3},{3,2},{4,5},{5,4},{6,7},{7,6},{8,9},{9,8},{10,11... | collective-permute-start | bytes 3932168 | tf_op jit(solution)/shard_map/ppermute | solution.py:866
  79.5 16.7 %collective-permute-start.10 = (bf16[1024,512]{1,0:T(8,128)(2,1)S(1)}, bf16[1024,512]{1,0:T(8,128)(2,1)S(1)}, u32[]{:S(2)}, u32[]{:S(2)}) collective-permute-start(bf16[1024,512]{1,0:T(8,128)(2,1)S(1)} %get-tuple-element.255), channel_id=1, source_target_pairs={{0,1},{1,0},{2,3},{3,2},{4,5},{5,4},{6,7},{7,6},{8,9},{9,8},{10,11... | collective-permute-start | bytes 3145736 | tf_op jit(solution)/shard_map/ppermute | solution.py:866
  80.0 16.2 %collective-permute-start.8 = (bf16[512,512]{1,0:T(8,128)(2,1)S(1)}, bf16[512,512]{1,0:T(8,128)(2,1)S(1)}, u32[]{:S(2)}, u32[]{:S(2)}) collective-permute-start(bf16[512,512]{1,0:T(8,128)(2,1)S(1)} %get-tuple-element.253), channel_id=1, source_target_pairs={{0,16},{16,0},{1,17},{17,1},{2,18},{18,2},{3,19},{19,3},{4,20},{20... | collective-permute-start | bytes 1572872 | tf_op jit(solution)/shard_map/ppermute | solution.py:866
  81.5 14.7 %collective-permute-start.11 = (bf16[256,512]{1,0:T(8,128)(2,1)S(1)}, bf16[256,512]{1,0:T(8,128)(2,1)S(1)}, u32[]{:S(2)}, u32[]{:S(2)}) collective-permute-start(bf16[256,512]{1,0:T(8,128)(2,1)S(1)} %get-tuple-element.256), channel_id=1, source_target_pairs={{0,4},{1,5},{2,6},{3,7},{4,0},{5,1},{6,2},{7,3},{8,12},{9,13},{10,... | collective-permute-start | bytes 786440 | tf_op jit(solution)/shard_map/ppermute | solution.py:866
  83.1 13.1 %collective-permute-start.12 = (bf16[256,512]{1,0:T(8,128)(2,1)S(1)}, bf16[256,512]{1,0:T(8,128)(2,1)S(1)}, u32[]{:S(2)}, u32[]{:S(2)}) collective-permute-start(bf16[256,512]{1,0:T(8,128)(2,1)S(1)} %get-tuple-element.257), channel_id=1, source_target_pairs={{0,2},{1,3},{2,0},{3,1},{4,6},{5,7},{6,4},{7,5},{8,10},{9,11},{10,... | collective-permute-start | bytes 786440 | tf_op jit(solution)/shard_map/ppermute | solution.py:866
  83.6 10.7 %copy-start.12 = (bf16[1024,512]{1,0:T(8,128)(2,1)S(1)}, bf16[1024,512]{1,0:T(8,128)(2,1)}, u32[]{:S(2)}) copy-start(bf16[1024,512]{1,0:T(8,128)(2,1)} %get-tuple-element.250.h_ref) | copy-start | bytes 3145732
  96.6 8.2 %collective-permute-start.14 = (bf16[768,512]{1,0:T(8,128)(2,1)S(1)}, bf16[768,512]{1,0:T(8,128)(2,1)S(1)}, u32[]{:S(2)}, u32[]{:S(2)}) collective-permute-start(bf16[768,512]{1,0:T(8,128)(2,1)S(1)} %get-tuple-element.285), channel_id=1, source_target_pairs={{0,1},{1,0},{2,3},{3,2},{4,5},{5,4},{6,7},{7,6},{8,9},{9,8},{10,11... | collective-permute-start | bytes 2359304 | tf_op jit(solution)/shard_map/ppermute | solution.py:866
  96.7 17.1 %collective-permute-start.19 = (bf16[640,512]{1,0:T(8,128)(2,1)S(1)}, bf16[640,512]{1,0:T(8,128)(2,1)S(1)}, u32[]{:S(2)}, u32[]{:S(2)}) collective-permute-start(bf16[640,512]{1,0:T(8,128)(2,1)S(1)} %get-tuple-element.297), channel_id=1, source_target_pairs={{0,2},{1,3},{2,0},{3,1},{4,6},{5,7},{6,4},{7,5},{8,10},{9,11},{10,... | collective-permute-start | bytes 1966088 | tf_op jit(solution)/shard_map/ppermute | solution.py:866
  98.3 14.0 %collective-permute-start.18 = (bf16[512,512]{1,0:T(8,128)(2,1)S(1)}, bf16[512,512]{1,0:T(8,128)(2,1)S(1)}, u32[]{:S(2)}, u32[]{:S(2)}) collective-permute-start(bf16[512,512]{1,0:T(8,128)(2,1)S(1)} %get-tuple-element.296), channel_id=1, source_target_pairs={{0,4},{1,5},{2,6},{3,7},{4,0},{5,1},{6,2},{7,3},{8,12},{9,13},{10,... | collective-permute-start | bytes 1572872 | tf_op jit(solution)/shard_map/ppermute | solution.py:866
  98.7 8.1 %collective-permute-start.13 = (bf16[256,512]{1,0:T(8,128)(2,1)S(1)}, bf16[256,512]{1,0:T(8,128)(2,1)S(1)}, u32[]{:S(2)}, u32[]{:S(2)}) collective-permute-start(bf16[256,512]{1,0:T(8,128)(2,1)S(1)} %get-tuple-element.283), channel_id=1, source_target_pairs={{0,16},{16,0},{1,17},{17,1},{2,18},{18,2},{3,19},{19,3},{4,20},{20... | collective-permute-start | bytes 786440 | tf_op jit(solution)/shard_map/ppermute | solution.py:866
  103.6 1.2 collective-permute-start.15
  104.9 14.2 %collective-permute-start.17 = (bf16[416,512]{1,0:T(8,128)(2,1)S(1)}, bf16[416,512]{1,0:T(8,128)(2,1)S(1)}, u32[]{:S(2)}, u32[]{:S(2)}) collective-permute-start(bf16[416,512]{1,0:T(8,128)(2,1)S(1)} %get-tuple-element.289), channel_id=1, source_target_pairs={{0,16},{16,0},{1,17},{17,1},{2,18},{18,2},{3,19},{19,3},{4,20},{20... | collective-permute-start | bytes 1277960 | tf_op jit(solution)/shard_map/ppermute | solution.py:866
  114.0 12.7 %collective-permute-start.23 = (bf16[320,512]{1,0:T(8,128)(2,1)S(1)}, bf16[320,512]{1,0:T(8,128)(2,1)S(1)}, u32[]{:S(2)}, u32[]{:S(2)}) collective-permute-start(bf16[320,512]{1,0:T(8,128)(2,1)S(1)} %get-tuple-element.306), channel_id=1, source_target_pairs={{0,16},{16,0},{1,17},{17,1},{2,18},{18,2},{3,19},{19,3},{4,20},{20... | collective-permute-start | bytes 983048 | tf_op jit(solution)/shard_map/ppermute | solution.py:866
  114.6 12.1 %collective-permute-start.21 = (bf16[256,512]{1,0:T(8,128)(2,1)S(1)}, bf16[256,512]{1,0:T(8,128)(2,1)S(1)}, u32[]{:S(2)}, u32[]{:S(2)}) collective-permute-start(bf16[256,512]{1,0:T(8,128)(2,1)S(1)} %get-tuple-element.311), channel_id=1, source_target_pairs={{0,4},{1,5},{2,6},{3,7},{4,0},{5,1},{6,2},{7,3},{8,12},{9,13},{10,... | collective-permute-start | bytes 786440 | tf_op jit(solution)/shard_map/ppermute | solution.py:866
  114.9 11.8 %collective-permute-start.22 = (bf16[256,512]{1,0:T(8,128)(2,1)S(1)}, bf16[256,512]{1,0:T(8,128)(2,1)S(1)}, u32[]{:S(2)}, u32[]{:S(2)}) collective-permute-start(bf16[256,512]{1,0:T(8,128)(2,1)S(1)} %get-tuple-element.312), channel_id=1, source_target_pairs={{0,2},{1,3},{2,0},{3,1},{4,6},{5,7},{6,4},{7,5},{8,10},{9,11},{10,... | collective-permute-start | bytes 786440 | tf_op jit(solution)/shard_map/ppermute | solution.py:866
  116.6 7.9 %collective-permute-start.16 = (bf16[128,512]{1,0:T(8,128)(2,1)S(1)}, bf16[128,512]{1,0:T(8,128)(2,1)S(1)}, u32[]{:S(2)}, u32[]{:S(2)}) collective-permute-start(bf16[128,512]{1,0:T(8,128)(2,1)S(1)} %get-tuple-element.292), channel_id=1, source_target_pairs={{0,8},{1,9},{2,10},{3,11},{4,12},{5,13},{6,14},{7,15},{8,0},{9,1},... | collective-permute-start | bytes 393224 | tf_op jit(solution)/shard_map/ppermute | solution.py:866
  119.2 13.3 %collective-permute-start.27 = (bf16[224,512]{1,0:T(8,128)(2,1)S(1)}, bf16[224,512]{1,0:T(8,128)(2,1)S(1)}, u32[]{:S(2)}, u32[]{:S(2)}) collective-permute-start(bf16[224,512]{1,0:T(8,128)(2,1)S(1)} %get-tuple-element.308), channel_id=1, source_target_pairs={{0,4},{1,5},{2,6},{3,7},{4,0},{5,1},{6,2},{7,3},{8,12},{9,13},{10,... | collective-permute-start | bytes 688136 | tf_op jit(solution)/shard_map/ppermute | solution.py:866
  126.8 9.2 %collective-permute-start.26 = (bf16[160,512]{1,0:T(8,128)(2,1)S(1)}, bf16[160,512]{1,0:T(8,128)(2,1)S(1)}, u32[]{:S(2)}, u32[]{:S(2)}) collective-permute-start(bf16[160,512]{1,0:T(8,128)(2,1)S(1)} %get-tuple-element.324), channel_id=1, source_target_pairs={{0,4},{1,5},{2,6},{3,7},{4,0},{5,1},{6,2},{7,3},{8,12},{9,13},{10,... | collective-permute-start | bytes 491528 | tf_op jit(solution)/shard_map/ppermute | solution.py:866
  129.5 5.0 %collective-permute-start.24 = (bf16[128,512]{1,0:T(8,128)(2,1)S(1)}, bf16[128,512]{1,0:T(8,128)(2,1)S(1)}, u32[]{:S(2)}, u32[]{:S(2)}) collective-permute-start(bf16[128,512]{1,0:T(8,128)(2,1)S(1)} %get-tuple-element.322), channel_id=1, source_target_pairs={{0,2},{1,3},{2,0},{3,1},{4,6},{5,7},{6,4},{7,5},{8,10},{9,11},{10,... | collective-permute-start | bytes 393224 | tf_op jit(solution)/shard_map/ppermute | solution.py:866
  131.0 5.0 %collective-permute-start.25 = (bf16[128,512]{1,0:T(8,128)(2,1)S(1)}, bf16[128,512]{1,0:T(8,128)(2,1)S(1)}, u32[]{:S(2)}, u32[]{:S(2)}) collective-permute-start(bf16[128,512]{1,0:T(8,128)(2,1)S(1)} %get-tuple-element.323), channel_id=1, source_target_pairs={{0,16},{16,0},{1,17},{17,1},{2,18},{18,2},{3,19},{19,3},{4,20},{20... | collective-permute-start | bytes 393224 | tf_op jit(solution)/shard_map/ppermute | solution.py:866
  132.5 6.5 %collective-permute-start.30 = (bf16[128,512]{1,0:T(8,128)(2,1)S(1)}, bf16[128,512]{1,0:T(8,128)(2,1)S(1)}, u32[]{:S(2)}, u32[]{:S(2)}) collective-permute-start(bf16[128,512]{1,0:T(8,128)(2,1)S(1)} %get-tuple-element.327), channel_id=1, source_target_pairs={{0,2},{1,3},{2,0},{3,1},{4,6},{5,7},{6,4},{7,5},{8,10},{9,11},{10,... | collective-permute-start | bytes 393224 | tf_op jit(solution)/shard_map/ppermute | solution.py:866
  136.0 11.2 %collective-permute-start.28 = (bf16[128,512]{1,0:T(8,128)(2,1)S(1)}, bf16[128,512]{1,0:T(8,128)(2,1)S(1)}, u32[]{:S(2)}, u32[]{:S(2)}) collective-permute-start(bf16[128,512]{1,0:T(8,128)(2,1)S(1)} %get-tuple-element.336), channel_id=1, source_target_pairs={{0,8},{1,9},{2,10},{3,11},{4,12},{5,13},{6,14},{7,15},{8,0},{9,1},... | collective-permute-start | bytes 393224 | tf_op jit(solution)/shard_map/ppermute | solution.py:866
  136.5 10.8 %collective-permute-start.29 = (bf16[80,512]{1,0:T(8,128)(2,1)S(1)}, bf16[80,512]{1,0:T(8,128)(2,1)S(1)}, u32[]{:S(2)}, u32[]{:S(2)}) collective-permute-start(bf16[80,512]{1,0:T(8,128)(2,1)S(1)} %get-tuple-element.337), channel_id=1, source_target_pairs={{0,8},{1,9},{2,10},{3,11},{4,12},{5,13},{6,14},{7,15},{8,0},{9,1},... | collective-permute-start | bytes 245768 | tf_op jit(solution)/shard_map/ppermute | solution.py:866
  139.0 10.3 %collective-permute-start.33 = (bf16[80,512]{1,0:T(8,128)(2,1)S(1)}, bf16[80,512]{1,0:T(8,128)(2,1)S(1)}, u32[]{:S(2)}, u32[]{:S(2)}) collective-permute-start(bf16[80,512]{1,0:T(8,128)(2,1)S(1)} %get-tuple-element.340), channel_id=1, source_target_pairs={{0,8},{1,9},{2,10},{3,11},{4,12},{5,13},{6,14},{7,15},{8,0},{9,1},... | collective-permute-start | bytes 245768 | tf_op jit(solution)/shard_map/ppermute | solution.py:866
  139.5 11.5 %collective-permute-start.20 = (bf16[128,512]{1,0:T(8,128)(2,1)S(1)}, bf16[128,512]{1,0:T(8,128)(2,1)S(1)}, u32[]{:S(2)}, u32[]{:S(2)}) collective-permute-start(bf16[128,512]{1,0:T(8,128)(2,1)S(1)} %shard_map.208.refs_0_), channel_id=1, source_target_pairs={{0,16},{16,0},{1,17},{17,1},{2,18},{18,2},{3,19},{19,3},{4,20},{20... | collective-permute-start | bytes 393224 | tf_op jit(solution)/shard_map/ppermute | solution.py:866
  147.3 6.0 %collective-permute-start.31 = (bf16[128,512]{1,0:T(8,128)(2,1)S(1)}, bf16[128,512]{1,0:T(8,128)(2,1)S(1)}, u32[]{:S(2)}, u32[]{:S(2)}) collective-permute-start(bf16[128,512]{1,0:T(8,128)(2,1)S(1)} %shard_map.215.refs_2_), channel_id=1, source_target_pairs={{0,16},{16,0},{1,17},{17,1},{2,18},{18,2},{3,19},{19,3},{4,20},{20... | collective-permute-start | bytes 393224 | tf_op jit(solution)/shard_map/ppermute | solution.py:866
  148.9 4.4 %collective-permute-start.32 = (bf16[80,512]{1,0:T(8,128)(2,1)S(1)}, bf16[80,512]{1,0:T(8,128)(2,1)S(1)}, u32[]{:S(2)}, u32[]{:S(2)}) collective-permute-start(bf16[80,512]{1,0:T(8,128)(2,1)S(1)} %shard_map.216.refs_4_), channel_id=1, source_target_pairs={{0,16},{16,0},{1,17},{17,1},{2,18},{18,2},{3,19},{19,3},{4,20},{20... | collective-permute-start | bytes 245768 | tf_op jit(solution)/shard_map/ppermute | solution.py:866
  149.4 4.8 %collective-permute-start.34 = (bf16[80,512]{1,0:T(8,128)(2,1)S(1)}, bf16[80,512]{1,0:T(8,128)(2,1)S(1)}, u32[]{:S(2)}, u32[]{:S(2)}) collective-permute-start(bf16[80,512]{1,0:T(8,128)(2,1)S(1)} %shard_map.217.refs_6_), channel_id=1, source_target_pairs={{0,16},{16,0},{1,17},{17,1},{2,18},{18,2},{3,19},{19,3},{4,20},{20... | collective-permute-start | bytes 245768 | tf_op jit(solution)/shard_map/ppermute | solution.py:866
  (1 other events, 3.1 us)
where the time goes:
time: 156 us
  Pallas kernels  88.7 us (57%)
  starting transfers between devices  36.1 us (23%)
  waiting for transfers between devices  28.8 us (18%)
    pallas_call x33, Pallas kernels, call(): pl.pallas_call(kernel, in_specs=[VMEM] * len(args) if specs is None else...  88.7 us
    ppermute x35, starting transfers between devices, swap(): return lax.ppermute(array, axis, [(i, i ^ 1 << bit) for i in range(size)])  36.1 us
    ppermute x35, waiting for transfers between devices, swap(): return lax.ppermute(array, axis, [(i, i ^ 1 << bit) for i in range(size)])  28.8 us
  transfers between devices with their start and end apart: 35, of which 13 were waited for; matrix products, arithmetic and copies ran while one was open for 1% of the time, Pallas kernels for 39%

commit v1 on v0

--- a/solution.py
+++ b/solution.py
@@ -883,7 +883,7 @@
 
     path_up1, path_down1 = (0, 1, 2, ROWS, 3), (0, 2, 1, ROWS, 3)
     path_attn1, path_down0 = (0, ROWS, 2, 1, 3), (0, 2, 1, ROWS, 3)
-    path_up0, path_qkv0 = (0, 1, ROWS, 2, 3), (0, ROWS, 2, 1, 3)
+    path_up0, path_qkv0 = (0, 1, ROWS, 3, 2), (0, ROWS, 2, 1, 3)
 
     def row_out(cols, dtype=BF16):
         return sds((rows, cols), dtype)

time: 156 us -> 153 us (0.981)
  starting transfers between devices: 36.1 us -> 34.5 us
    ppermute x35, starting transfers between devices: 36.1 us -> 34.5 us  [swap(): return lax.ppermute(array, axis, [(i, i ^ 1 << bit) for i in range(size)])]
  transfers between devices with their start and end apart: 35 -> 35, of which waited for: 13 -> 15; matrix products, arithmetic and copies ran while one was open for 1% -> 1% of each run, Pallas kernels for 39% -> 40%
where the time goes in v1:
time: 153 us
  Pallas kernels  88.7 us (58%)
  starting transfers between devices  34.5 us (23%)
  waiting for transfers between devices  27.7 us (18%)
    pallas_call x33, Pallas kernels, call(): pl.pallas_call(kernel, in_specs=[VMEM] * len(args) if specs is None else...  88.7 us
    ppermute x35, starting transfers between devices, swap(): return lax.ppermute(array, axis, [(i, i ^ 1 << bit) for i in range(size)])  34.5 us
    ppermute x35, waiting for transfers between devices, swap(): return lax.ppermute(array, axis, [(i, i ^ 1 << bit) for i in range(size)])  27.7 us
  transfers between devices with their start and end apart: 35, of which 15 were waited for; matrix products, arithmetic and copies ran while one was open for 1% of the time, Pallas kernels for 40%

profile of v1, /device:TPU:0, one launch (start us, length us, event | category | flops | bytes accessed | tf_op | source)
XLA Modules:
  0.0 153.1 jit_solution(8395796866021729579)
XLA Ops:
  0.6 0.5 collective-permute-start.1
  1.2 0.8 select_maximum_fusion.params_ref
  2.0 20.9 %shard_map.186 = (bf16[4,128,512]{2,1,0:T(8,128)(2,1)S(1)}, bf16[4,128,512]{2,1,0:T(8,128)(2,1)S(1)}, bf16[1024,512]{1,0:T(8,128)(2,1)}, bf16[1024,1536]{1,0:T(8...) custom-call(bf16[4,256,512]{2,1,0:T(8,128)(2,1)} %tok_ref.1, ...), custom_call_target="tpu_custom_call" | custom-call | flops 368000000 | tf_op jit(solution)/shard_map/pallas_call | solution.py:854
  23.0 1.9 %collective-permute-done.recv_ref = bf16[4,128,512]{2,1,0:T(8,128)(2,1)S(1)} collective-permute-done((bf16[4,128,512]{2,1,0:T(8,128)(2,1)S(1)}, bf16[4,128,512]{2,1,0:T(8,128)(2,1)S(1)}, u32[]{:S(2)}, u32[]{:S(2)}) %collective-permute-start) | collective-permute-done | bytes 524320 | tf_op jit(solution)/shard_map/ppermute | solution.py:866
  24.9 21.2 %shard_map.187 = (bf16[4,128,512]{2,1,0:T(8,128)(2,1)S(1)}, bf16[4,128,512]{2,1,0:T(8,128)(2,1)S(1)}, bf16[1024,512]{1,0:T(8,128)(2,1)S(1)}, bf16[1024,512]{1,0:...) custom-call(s32[8,8]{1,0:T(8,128)S(1)} %copy-done.13, ...), custom_call_target="tpu_custom_call" | custom-call | flops 552000000 | tf_op jit(solution)/shard_map/pallas_call | solution.py:854
  46.0 4.6 %shard_map.188 = (bf16[2048,512]{1,0:T(8,128)(2,1)S(1)}, bf16[2048,512]{1,0:T(8,128)(2,1)S(1)}) custom-call(bf16[1024,512]{1,0:T(8,128)(2,1)S(1)} %get-tuple-element.188.h_ref, bf16[1024,2048]{1,0:T(8,128)(2,1)S(1)} %get-tuple-element.189.du_ref, bf16[1024,2048]{1,0:T(8,128)(2,1)S(1)} %get-tuple-element.190.act_ref, ...), custom_call_target="tpu_custom_call" | custom-call | flops 103500000 | tf_op jit(solution)/shard_map/pallas_call | solution.py:854
  51.2 8.0 %shard_map.189 = (bf16[4,128,512]{2,1,0:T(8,128)(2,1)S(1)}, bf16[4,128,512]{2,1,0:T(8,128)(2,1)S(1)}, bf16[1024,512]{1,0:T(8,128)(2,1)S(1)}, bf16[1024,1536]{1,0:T(8,128)(2,1)S(1)}, f32[8,512]{1,0:T(8,128)S(1)}) custom-call(s32[8,8]{1,0:T(8,128)S(1)} %copy-done.13, bf16[1024,512]{1,0:T(8,128)(2,1)S(1)} %get-tuple-element.186.x_ref, ...), custom_call_target="tpu_custom_call" | custom-call | flops 184000000 | tf_op jit(solution)/shard_map/pallas_call | solution.py:854
  59.4 2.4 %shard_map.190 = (bf16[1024,512]{1,0:T(8,128)(2,1)S(1)}, bf16[1024,512]{1,0:T(8,128)(2,1)S(1)}) custom-call(bf16[1024,512]{1,0:T(8,128)(2,1)S(1)} %get-tuple-element.200.h_ref, bf16[1024,1536]{1,0:T(8,128)(2,1)S(1)} %get-tuple-element.201.dqkv_ref, bf16[1024,512]{1,0:T(8,128)(2,1)S(1)} %get-tuple-element.202.o_ref, ...), custom_call_target="tpu_custom_call" | custom-call | flops 55200000 | tf_op jit(solution)/shard_map/pallas_call | solution.py:854
  62.6 2.6 %collective-permute-start.5 = (bf16[512,512]{1,0:T(8,128)(2,1)S(1)}, bf16[512,512]{1,0:T(8,128)(2,1)S(1)}, u32[]{:S(2)}, u32[]{:S(2)}) collective-permute-start(bf16[512,512]{1,0:T(8,128)(2,1)S(1)} %get-tuple-element.230), channel_id=1, source_target_pairs={{0,2},{1,3},{2,0},{3,1},{4,6},{5,7},{6,4},{7,5},{8,10},{9,11},{10,... | collective-permute-start | bytes 1572872 | tf_op jit(solution)/shard_map/ppermute | solution.py:866
  65.2 1.6 %collective-permute-start.6 = (bf16[512,512]{1,0:T(8,128)(2,1)S(1)}, bf16[512,512]{1,0:T(8,128)(2,1)S(1)}, u32[]{:S(2)}, u32[]{:S(2)}) collective-permute-start(bf16[512,512]{1,0:T(8,128)(2,1)S(1)} %get-tuple-element.231), channel_id=1, source_target_pairs={{0,4},{1,5},{2,6},{3,7},{4,0},{5,1},{6,2},{7,3},{8,12},{9,13},{10,... | collective-permute-start | bytes 1572872 | tf_op jit(solution)/shard_map/ppermute | solution.py:866
  66.8 2.4 %shard_map.192 = (bf16[1024,512]{1,0:T(8,128)(2,1)S(1)}, bf16[1024,512]{1,0:T(8,128)(2,1)S(1)}, bf16[1024,512]{1,0:T(8,128)(2,1)S(1)}) custom-call(bf16[1024,2048]{1,0:T(8,128)(2,1)S(1)} %copy-done.5, bf16[4,128,512]{2,1,0:T(8,128)(2,1)S(1)} %get-tuple-element.217.own_ref, bf16[4,128,512]{2,1,0:T(8,128)(2,1)S(1)} %collective-permute-done.2.recv_ref), custom_call_target="tpu_custom_call" | custom-call | flops 55200000 | tf_op jit(solution)/shard_map/pallas_call | solution.py:854
  69.3 6.6 %shard_map.193 = (bf16[1024,2048]{1,0:T(8,128)(2,1)S(1)}, f32[1024,512]{1,0:T(8,128)S(1)}, bf16[1024,512]{1,0:T(8,128)(2,1)S(1)}, f32[8,512]{1,0:T(8,128)S(1)}) custom-call(bf16[1024,512]{1,0:T(8,128)(2,1)S(1)} %get-tuple-element.222.gr_ref, f32[1024,512]{1,0:T(8,128)S(1)} %copy-done.9, bf16[1024,2048]{1,0:T(8,128)(2,1)S(1)} %copy-done.6, ...), custom_call_target="tpu_custom_call" | custom-call | flops 138000000 | tf_op jit(solution)/shard_map/pallas_call | solution.py:854
  75.9 2.9 %shard_map.194 = (bf16[1280,512]{1,0:T(8,128)(2,1)S(1)}, bf16[1280,512]{1,0:T(8,128)(2,1)S(1)}) custom-call(bf16[1024,512]{1,0:T(8,128)(2,1)S(1)} %copy-done.11, bf16[1024,2048]{1,0:T(8,128)(2,1)S(1)} %get-tuple-element.225.du_ref, bf16[1024,512]{1,0:T(8,128)(2,1)S(1)} %copy-done.4, bf16[1024,512]{1,0:T(8,128)(2,1)S(1)} %get-tuple-element.247.ar_ref), custom_call_target="tpu_custom_call" | custom-call | flops 69000000 | tf_op jit(solution)/shard_map/pallas_call | solution.py:854
  79.5 0.5 collective-permute-start.10
  80.0 1.5 %collective-permute-start.8 = (bf16[512,512]{1,0:T(8,128)(2,1)S(1)}, bf16[512,512]{1,0:T(8,128)(2,1)S(1)}, u32[]{:S(2)}, u32[]{:S(2)}) collective-permute-start(bf16[512,512]{1,0:T(8,128)(2,1)S(1)} %get-tuple-element.253), channel_id=1, source_target_pairs={{0,16},{16,0},{1,17},{17,1},{2,18},{18,2},{3,19},{19,3},{4,20},{20... | collective-permute-start | bytes 1572872 | tf_op jit(solution)/shard_map/ppermute | solution.py:866
  81.5 1.6 %collective-permute-start.11 = (bf16[256,512]{1,0:T(8,128)(2,1)S(1)}, bf16[256,512]{1,0:T(8,128)(2,1)S(1)}, u32[]{:S(2)}, u32[]{:S(2)}) collective-permute-start(bf16[256,512]{1,0:T(8,128)(2,1)S(1)} %get-tuple-element.256), channel_id=1, source_target_pairs={{0,4},{1,5},{2,6},{3,7},{4,0},{5,1},{6,2},{7,3},{8,12},{9,13},{10,... | collective-permute-start | bytes 786440 | tf_op jit(solution)/shard_map/ppermute | solution.py:866
  83.1 0.5 collective-permute-start.12
  83.6 10.7 %shard_map.197.dqkv_ref = bf16[1024,1536]{1,0:T(8,128)(2,1)S(1)} custom-call(bf16[1024,512]{1,0:T(8,128)(2,1)S(1)} %get-tuple-element.247.ar_ref, bf16[1024,1536]{1,0:T(8,128)(2,1)S(1)} %copy-done.8, f32[4,8,256]{2,1,0:T(8,128)S(1)} %get-tuple-element.249.lse_ref, bf16[1024,512]{1,0:T(8,128)(2,1)S(1)} %copy-done.4, bf16[2,512,512]{2,1,0:T(8,128)(2,1)S(1)} %copy-done.3), custom_call_target="tpu_custom_call" | custom-call | flops 230000000 | tf_op jit(solution)/shard_map/pallas_call | solution.py:854
  94.3 1.8 %shard_map.198 = (bf16[768,512]{1,0:T(8,128)(2,1)S(1)}, bf16[768,512]{1,0:T(8,128)(2,1)S(1)}) custom-call(bf16[1024,1536]{1,0:T(8,128)(2,1)S(1)} %shard_map.197.dqkv_ref, bf16[1024,512]{1,0:T(8,128)(2,1)S(1)} %copy-done.12), custom_call_target="tpu_custom_call" | custom-call | flops 46000000 | tf_op jit(solution)/shard_map/pallas_call | solution.py:854
  96.7 1.6 %collective-permute-start.19 = (bf16[640,512]{1,0:T(8,128)(2,1)S(1)}, bf16[640,512]{1,0:T(8,128)(2,1)S(1)}, u32[]{:S(2)}, u32[]{:S(2)}) collective-permute-start(bf16[640,512]{1,0:T(8,128)(2,1)S(1)} %get-tuple-element.297), channel_id=1, source_target_pairs={{0,2},{1,3},{2,0},{3,1},{4,6},{5,7},{6,4},{7,5},{8,10},{9,11},{10,... | collective-permute-start | bytes 1966088 | tf_op jit(solution)/shard_map/ppermute | solution.py:866
  98.3 0.5 collective-permute-start.18
  98.7 0.5 collective-permute-start.13
  99.2 4.4 %shard_map.202 = (bf16[4,256,512]{2,1,0:T(8,128)(2,1)}, bf16[4,256,512]{2,1,0:T(8,128)(2,1)}, bf16[32,512]{1,0:T(8,128)(2,1)S(1)}) custom-call(bf16[1024,1536]{1,0:T(8,128)(2,1)S(1)} %shard_map.197.dqkv_ref, bf16[4,256,512]{2,1,0:T(8,128)(2,1)S(1)} %copy-done.7, f32[1024,512]{1,0:T(8,128)S(1)} %get-tuple-element.274.dxa_ref, ...), custom_call_target="tpu_custom_call" | custom-call | flops 92000000 | tf_op jit(solution)/shard_map/pallas_call | solution.py:854
  103.6 1.2 collective-permute-done.15.refs_3_
  104.9 1.6 %collective-permute-start.17 = (bf16[416,512]{1,0:T(8,128)(2,1)S(1)}, bf16[416,512]{1,0:T(8,128)(2,1)S(1)}, u32[]{:S(2)}, u32[]{:S(2)}) collective-permute-start(bf16[416,512]{1,0:T(8,128)(2,1)S(1)} %get-tuple-element.289), channel_id=1, source_target_pairs={{0,16},{16,0},{1,17},{17,1},{2,18},{18,2},{3,19},{19,3},{4,20},{20... | collective-permute-start | bytes 1277960 | tf_op jit(solution)/shard_map/ppermute | solution.py:866
  106.9 5.4 %collective-permute-done.18.refs_3_ = bf16[512,512]{1,0:T(8,128)(2,1)S(1)} collective-permute-done((bf16[512,512]{1,0:T(8,128)(2,1)S(1)}, bf16[512,512]{1,0:T(8,128)(2,1)S(1)}, u32[]{:S(2)}, u32[]{:S(2)}) %collective-permute-start.18) | collective-permute-done | bytes 524320 | tf_op jit(solution)/shard_map/ppermute | solution.py:866
  112.3 1.6 %collective-permute-done.19.refs_1_ = bf16[640,512]{1,0:T(8,128)(2,1)S(1)} collective-permute-done((bf16[640,512]{1,0:T(8,128)(2,1)S(1)}, bf16[640,512]{1,0:T(8,128)(2,1)S(1)}, u32[]{:S(2)}, u32[]{:S(2)}) %collective-permute-start.19) | collective-permute-done | bytes 655392 | tf_op jit(solution)/shard_map/ppermute | solution.py:866
  114.0 0.6 collective-permute-start.23
  114.9 1.7 %collective-permute-start.22 = (bf16[256,512]{1,0:T(8,128)(2,1)S(1)}, bf16[256,512]{1,0:T(8,128)(2,1)S(1)}, u32[]{:S(2)}, u32[]{:S(2)}) collective-permute-start(bf16[256,512]{1,0:T(8,128)(2,1)S(1)} %get-tuple-element.312), channel_id=1, source_target_pairs={{0,2},{1,3},{2,0},{3,1},{4,6},{5,7},{6,4},{7,5},{8,10},{9,11},{10,... | collective-permute-start | bytes 786440 | tf_op jit(solution)/shard_map/ppermute | solution.py:866
  116.6 2.6 %collective-permute-start.16 = (bf16[128,512]{1,0:T(8,128)(2,1)S(1)}, bf16[128,512]{1,0:T(8,128)(2,1)S(1)}, u32[]{:S(2)}, u32[]{:S(2)}) collective-permute-start(bf16[128,512]{1,0:T(8,128)(2,1)S(1)} %get-tuple-element.292), channel_id=1, source_target_pairs={{0,8},{1,9},{2,10},{3,11},{4,12},{5,13},{6,14},{7,15},{8,0},{9,1},... | collective-permute-start | bytes 393224 | tf_op jit(solution)/shard_map/ppermute | solution.py:866
  119.2 1.7 %collective-permute-start.27 = (bf16[224,512]{1,0:T(8,128)(2,1)S(1)}, bf16[224,512]{1,0:T(8,128)(2,1)S(1)}, u32[]{:S(2)}, u32[]{:S(2)}) collective-permute-start(bf16[224,512]{1,0:T(8,128)(2,1)S(1)} %get-tuple-element.308), channel_id=1, source_target_pairs={{0,4},{1,5},{2,6},{3,7},{4,0},{5,1},{6,2},{7,3},{8,12},{9,13},{10,... | collective-permute-start | bytes 688136 | tf_op jit(solution)/shard_map/ppermute | solution.py:866
  120.9 3.6 %collective-permute-done.16.refs_1_ = bf16[128,512]{1,0:T(8,128)(2,1)S(1)} collective-permute-done((bf16[128,512]{1,0:T(8,128)(2,1)S(1)}, bf16[128,512]{1,0:T(8,128)(2,1)S(1)}, u32[]{:S(2)}, u32[]{:S(2)}) %collective-permute-start.16) | collective-permute-done | bytes 131104 | tf_op jit(solution)/shard_map/ppermute | solution.py:866
  124.5 2.2 %collective-permute-done.21.refs_1_ = bf16[256,512]{1,0:T(8,128)(2,1)S(1)} collective-permute-done((bf16[256,512]{1,0:T(8,128)(2,1)S(1)}, bf16[256,512]{1,0:T(8,128)(2,1)S(1)}, u32[]{:S(2)}, u32[]{:S(2)}) %collective-permute-start.21) | collective-permute-done | bytes 262176 | tf_op jit(solution)/shard_map/ppermute | solution.py:866
  126.8 1.3 collective-permute-start.26
  128.1 1.7 %collective-permute-start.24 = (bf16[128,512]{1,0:T(8,128)(2,1)S(1)}, bf16[128,512]{1,0:T(8,128)(2,1)S(1)}, u32[]{:S(2)}, u32[]{:S(2)}) collective-permute-start(bf16[128,512]{1,0:T(8,128)(2,1)S(1)} %get-tuple-element.322), channel_id=1, source_target_pairs={{0,2},{1,3},{2,0},{3,1},{4,6},{5,7},{6,4},{7,5},{8,10},{9,11},{10,... | collective-permute-start | bytes 393224 | tf_op jit(solution)/shard_map/ppermute | solution.py:866
  129.7 1.5 %collective-permute-start.25 = (bf16[128,512]{1,0:T(8,128)(2,1)S(1)}, bf16[128,512]{1,0:T(8,128)(2,1)S(1)}, u32[]{:S(2)}, u32[]{:S(2)}) collective-permute-start(bf16[128,512]{1,0:T(8,128)(2,1)S(1)} %get-tuple-element.323), channel_id=1, source_target_pairs={{0,16},{16,0},{1,17},{17,1},{2,18},{18,2},{3,19},{19,3},{4,20},{20... | collective-permute-start | bytes 393224 | tf_op jit(solution)/shard_map/ppermute | solution.py:866
  131.3 0.8 collective-permute-done.27.refs_1_
  132.1 1.7 %collective-permute-start.30 = (bf16[128,512]{1,0:T(8,128)(2,1)S(1)}, bf16[128,512]{1,0:T(8,128)(2,1)S(1)}, u32[]{:S(2)}, u32[]{:S(2)}) collective-permute-start(bf16[128,512]{1,0:T(8,128)(2,1)S(1)} %get-tuple-element.327), channel_id=1, source_target_pairs={{0,2},{1,3},{2,0},{3,1},{4,6},{5,7},{6,4},{7,5},{8,10},{9,11},{10,... | collective-permute-start | bytes 393224 | tf_op jit(solution)/shard_map/ppermute | solution.py:866
  133.8 0.9 collective-permute-done.25.refs_3_
  134.7 1.8 %collective-permute-done.26.refs_1_ = bf16[160,512]{1,0:T(8,128)(2,1)S(1)} collective-permute-done((bf16[160,512]{1,0:T(8,128)(2,1)S(1)}, bf16[160,512]{1,0:T(8,128)(2,1)S(1)}, u32[]{:S(2)}, u32[]{:S(2)}) %collective-permute-start.26) | collective-permute-done | bytes 163872 | tf_op jit(solution)/shard_map/ppermute | solution.py:866
  136.7 2.3 %collective-permute-start.29 = (bf16[80,512]{1,0:T(8,128)(2,1)S(1)}, bf16[80,512]{1,0:T(8,128)(2,1)S(1)}, u32[]{:S(2)}, u32[]{:S(2)}) collective-permute-start(bf16[80,512]{1,0:T(8,128)(2,1)S(1)} %get-tuple-element.337), channel_id=1, source_target_pairs={{0,4},{1,5},{2,6},{3,7},{4,0},{5,1},{6,2},{7,3},{8,12},{9,13},{10,... | collective-permute-start | bytes 245768 | tf_op jit(solution)/shard_map/ppermute | solution.py:866
  139.0 0.6 collective-permute-start.33
  139.7 1.6 %collective-permute-start.20 = (bf16[128,512]{1,0:T(8,128)(2,1)S(1)}, bf16[128,512]{1,0:T(8,128)(2,1)S(1)}, u32[]{:S(2)}, u32[]{:S(2)}) collective-permute-start(bf16[128,512]{1,0:T(8,128)(2,1)S(1)} %shard_map.208.refs_0_), channel_id=1, source_target_pairs={{0,16},{16,0},{1,17},{17,1},{2,18},{18,2},{3,19},{19,3},{4,20},{20... | collective-permute-start | bytes 393224 | tf_op jit(solution)/shard_map/ppermute | solution.py:866
  141.4 3.2 %collective-permute-done.28.refs_1_ = bf16[128,512]{1,0:T(8,128)(2,1)S(1)} collective-permute-done((bf16[128,512]{1,0:T(8,128)(2,1)S(1)}, bf16[128,512]{1,0:T(8,128)(2,1)S(1)}, u32[]{:S(2)}, u32[]{:S(2)}) %collective-permute-start.28) | collective-permute-done | bytes 131104 | tf_op jit(solution)/shard_map/ppermute | solution.py:866
  145.2 1.6 %collective-permute-start.32 = (bf16[80,512]{1,0:T(8,128)(2,1)S(1)}, bf16[80,512]{1,0:T(8,128)(2,1)S(1)}, u32[]{:S(2)}, u32[]{:S(2)}) collective-permute-start(bf16[80,512]{1,0:T(8,128)(2,1)S(1)} %shard_map.216.refs_4_), channel_id=1, source_target_pairs={{0,16},{16,0},{1,17},{17,1},{2,18},{18,2},{3,19},{19,3},{4,20},{20... | collective-permute-start | bytes 245768 | tf_op jit(solution)/shard_map/ppermute | solution.py:866
  147.3 3.4 %collective-permute-done.32.refs_5_ = bf16[80,512]{1,0:T(8,128)(2,1)S(1)} collective-permute-done((bf16[80,512]{1,0:T(8,128)(2,1)S(1)}, bf16[80,512]{1,0:T(8,128)(2,1)S(1)}, u32[]{:S(2)}, u32[]{:S(2)}) %collective-permute-start.32) | collective-permute-done | bytes 81952 | tf_op jit(solution)/shard_map/ppermute | solution.py:866
  150.6 0.9 collective-permute-done.34.refs_7_
  151.5 1.4 shard_map.218
  (84 shorter events, 5.2 us)
Async XLA Ops:
  0.6 24.2 %collective-permute-start.1 = (bf16[4,256,512]{2,1,0:T(8,128)(2,1)}, bf16[4,256,512]{2,1,0:T(8,128)(2,1)S(1)}, u32[]{:S(2)}, u32[]{:S(2)}) collective-permute-start(bf16[4,256,512]{2,1,0:T(8,128)(2,1)} %cot_ref.1), channel_id=1, source_target_pairs={{0,1},{1,0},{2,3},{3,2},{4,5},{5,4},{6,7},{7,6},{8,9},{9,8},{10,11... | collective-permute-start | bytes 3145736 | tf_op jit(solution)/shard_map/ppermute | solution.py:866
  1.9 22.9 %copy-start.2 = (bf16[2,512,1536]{2,1,0:T(8,128)(2,1)S(1)}, bf16[2,512,1536]{2,1,0:T(8,128)(2,1)}, u32[]{:S(2)}) copy-start(bf16[2,512,1536]{2,1,0:T(8,128)(2,1)} %wqkv_ref.1) | copy-start | bytes 9437188
  2.0 22.9 %copy-start.3 = (bf16[2,512,512]{2,1,0:T(8,128)(2,1)S(1)}, bf16[2,512,512]{2,1,0:T(8,128)(2,1)}, u32[]{:S(2)}) copy-start(bf16[2,512,512]{2,1,0:T(8,128)(2,1)} %wout_ref.1) | copy-start | bytes 3145732
  2.0 22.9 %copy-start.10 = (bf16[4,256,512]{2,1,0:T(8,128)(2,1)S(1)}, bf16[4,256,512]{2,1,0:T(8,128)(2,1)}, u32[]{:S(2)}) copy-start(bf16[4,256,512]{2,1,0:T(8,128)(2,1)} %cot_ref.1) | copy-start | bytes 3145732
  2.0 22.9 %copy-start.13 = (s32[8,8]{1,0:T(8,128)S(1)}, s32[8,8]{1,0:T(8,128)}, u32[]{:S(2)}) copy-start(s32[8,8]{1,0:T(8,128)} %slots_ref.3) | copy-start | bytes 772
  22.9 2.0 %collective-permute-start = (bf16[4,128,512]{2,1,0:T(8,128)(2,1)S(1)}, bf16[4,128,512]{2,1,0:T(8,128)(2,1)S(1)}, u32[]{:S(2)}, u32[]{:S(2)}) collective-permute-start(bf16[4,128,512]{2,1,0:T(8,128)(2,1)S(1)} %get-tuple-element.185), channel_id=1, source_target_pairs={{0,1},{1,0},{2,3},{3,2},{4,5},{5,4},{6,7},{7,6},{8,9},{9,8},{10,11... | collective-permute-start | bytes 1572872 | tf_op jit(solution)/shard_map/ppermute | solution.py:866
  50.6 11.2 %collective-permute-start.4 = (bf16[2048,512]{1,0:T(8,128)(2,1)S(1)}, bf16[2048,512]{1,0:T(8,128)(2,1)S(1)}, u32[]{:S(2)}, u32[]{:S(2)}) collective-permute-start(bf16[2048,512]{1,0:T(8,128)(2,1)S(1)} %get-tuple-element.207), channel_id=1, source_target_pairs={{0,1},{1,0},{2,3},{3,2},{4,5},{5,4},{6,7},{7,6},{8,9},{9,8},{10,11... | collective-permute-start | bytes 6291464 | tf_op jit(solution)/shard_map/ppermute | solution.py:866
  50.8 11.0 %collective-permute-start.3 = (bf16[4,128,512]{2,1,0:T(8,128)(2,1)S(1)}, bf16[4,128,512]{2,1,0:T(8,128)(2,1)S(1)}, u32[]{:S(2)}, u32[]{:S(2)}) collective-permute-start(bf16[4,128,512]{2,1,0:T(8,128)(2,1)S(1)} %get-tuple-element.206), channel_id=1, source_target_pairs={{0,1},{1,0},{2,3},{3,2},{4,5},{5,4},{6,7},{7,6},{8,9},{9,8},{10,11... | collective-permute-start | bytes 1572872 | tf_op jit(solution)/shard_map/ppermute | solution.py:866
  51.2 18.0 %copy-start.6 = (bf16[1024,2048]{1,0:T(8,128)(2,1)S(1)}, bf16[1024,2048]{1,0:T(8,128)(2,1)}, u32[]{:S(2)}) copy-start(bf16[1024,2048]{1,0:T(8,128)(2,1)} %get-tuple-element.224.slope_ref) | copy-start | bytes 12582916
  59.2 2.6 %collective-permute-start.2 = (bf16[4,128,512]{2,1,0:T(8,128)(2,1)S(1)}, bf16[4,128,512]{2,1,0:T(8,128)(2,1)S(1)}, u32[]{:S(2)}, u32[]{:S(2)}) collective-permute-start(bf16[4,128,512]{2,1,0:T(8,128)(2,1)S(1)} %get-tuple-element.199), channel_id=1, source_target_pairs={{0,1},{1,0},{2,3},{3,2},{4,5},{5,4},{6,7},{7,6},{8,9},{9,8},{10,11... | collective-permute-start | bytes 1572872 | tf_op jit(solution)/shard_map/ppermute | solution.py:866
  59.4 7.4 %copy-start.5 = (bf16[1024,2048]{1,0:T(8,128)(2,1)S(1)}, bf16[1024,2048]{1,0:T(8,128)(2,1)}, u32[]{:S(2)}) copy-start(bf16[1024,2048]{1,0:T(8,128)(2,1)} %get-tuple-element.183.act_ref) | copy-start | bytes 12582916
  59.4 9.8 %copy-start.9 = (f32[1024,512]{1,0:T(8,128)S(1)}, f32[1024,512]{1,0:T(8,128)}, u32[]{:S(2)}) copy-start(f32[1024,512]{1,0:T(8,128)} %get-tuple-element.223.xa_ref) | copy-start | bytes 6291460
  61.8 7.4 %copy-start.1 = (bf16[2,2048,512]{2,1,0:T(8,128)(2,1)S(1)}, bf16[2,2048,512]{2,1,0:T(8,128)(2,1)}, u32[]{:S(2)}) copy-start(bf16[2,2048,512]{2,1,0:T(8,128)(2,1)} %wdown_ref.1) | copy-start | bytes 12582916
  62.2 7.1 %copy-start = (bf16[2,512,2048]{2,1,0:T(8,128)(2,1)S(1)}, bf16[2,512,2048]{2,1,0:T(8,128)(2,1)}, u32[]{:S(2)}) copy-start(bf16[2,512,2048]{2,1,0:T(8,128)(2,1)} %wup_ref.1) | copy-start | bytes 12582916
  62.2 17.0 %collective-permute-start.7 = (bf16[1024,512]{1,0:T(8,128)(2,1)S(1)}, bf16[1024,512]{1,0:T(8,128)(2,1)S(1)}, u32[]{:S(2)}, u32[]{:S(2)}) collective-permute-start(bf16[1024,512]{1,0:T(8,128)(2,1)S(1)} %get-tuple-element.232), channel_id=1, source_target_pairs={{0,1},{1,0},{2,3},{3,2},{4,5},{5,4},{6,7},{7,6},{8,9},{9,8},{10,11... | collective-permute-start | bytes 3145736 | tf_op jit(solution)/shard_map/ppermute | solution.py:866
  62.6 16.2 %collective-permute-start.5 = (bf16[512,512]{1,0:T(8,128)(2,1)S(1)}, bf16[512,512]{1,0:T(8,128)(2,1)S(1)}, u32[]{:S(2)}, u32[]{:S(2)}) collective-permute-start(bf16[512,512]{1,0:T(8,128)(2,1)S(1)} %get-tuple-element.230), channel_id=1, source_target_pairs={{0,2},{1,3},{2,0},{3,1},{4,6},{5,7},{6,4},{7,5},{8,10},{9,11},{10,... | collective-permute-start | bytes 1572872 | tf_op jit(solution)/shard_map/ppermute | solution.py:866
  65.2 13.9 %collective-permute-start.6 = (bf16[512,512]{1,0:T(8,128)(2,1)S(1)}, bf16[512,512]{1,0:T(8,128)(2,1)S(1)}, u32[]{:S(2)}, u32[]{:S(2)}) collective-permute-start(bf16[512,512]{1,0:T(8,128)(2,1)S(1)} %get-tuple-element.231), channel_id=1, source_target_pairs={{0,4},{1,5},{2,6},{3,7},{4,0},{5,1},{6,2},{7,3},{8,12},{9,13},{10,... | collective-permute-start | bytes 1572872 | tf_op jit(solution)/shard_map/ppermute | solution.py:866
  69.3 6.6 %copy-start.4 = (bf16[1024,512]{1,0:T(8,128)(2,1)S(1)}, bf16[1024,512]{1,0:T(8,128)(2,1)}, u32[]{:S(2)}) copy-start(bf16[1024,512]{1,0:T(8,128)(2,1)} %get-tuple-element.226.o_ref) | copy-start | bytes 3145732
  69.3 6.6 %copy-start.11 = (bf16[1024,512]{1,0:T(8,128)(2,1)S(1)}, bf16[1024,512]{1,0:T(8,128)(2,1)}, u32[]{:S(2)}) copy-start(bf16[1024,512]{1,0:T(8,128)(2,1)} %get-tuple-element.221.h_ref) | copy-start | bytes 3145732
  78.8 4.8 %copy-start.8 = (bf16[1024,1536]{1,0:T(8,128)(2,1)S(1)}, bf16[1024,1536]{1,0:T(8,128)(2,1)}, u32[]{:S(2)}) copy-start(bf16[1024,1536]{1,0:T(8,128)(2,1)} %get-tuple-element.248.qkv_ref) | copy-start | bytes 9437188
  79.4 16.8 %collective-permute-start.9 = (bf16[1280,512]{1,0:T(8,128)(2,1)S(1)}, bf16[1280,512]{1,0:T(8,128)(2,1)S(1)}, u32[]{:S(2)}, u32[]{:S(2)}) collective-permute-start(bf16[1280,512]{1,0:T(8,128)(2,1)S(1)} %get-tuple-element.254), channel_id=1, source_target_pairs={{0,1},{1,0},{2,3},{3,2},{4,5},{5,4},{6,7},{7,6},{8,9},{9,8},{10,11... | collective-permute-start | bytes 3932168 | tf_op jit(solution)/shard_map/ppermute | solution.py:866
  79.5 16.7 %collective-permute-start.10 = (bf16[1024,512]{1,0:T(8,128)(2,1)S(1)}, bf16[1024,512]{1,0:T(8,128)(2,1)S(1)}, u32[]{:S(2)}, u32[]{:S(2)}) collective-permute-start(bf16[1024,512]{1,0:T(8,128)(2,1)S(1)} %get-tuple-element.255), channel_id=1, source_target_pairs={{0,1},{1,0},{2,3},{3,2},{4,5},{5,4},{6,7},{7,6},{8,9},{9,8},{10,11... | collective-permute-start | bytes 3145736 | tf_op jit(solution)/shard_map/ppermute | solution.py:866
  80.0 16.2 %collective-permute-start.8 = (bf16[512,512]{1,0:T(8,128)(2,1)S(1)}, bf16[512,512]{1,0:T(8,128)(2,1)S(1)}, u32[]{:S(2)}, u32[]{:S(2)}) collective-permute-start(bf16[512,512]{1,0:T(8,128)(2,1)S(1)} %get-tuple-element.253), channel_id=1, source_target_pairs={{0,16},{16,0},{1,17},{17,1},{2,18},{18,2},{3,19},{19,3},{4,20},{20... | collective-permute-start | bytes 1572872 | tf_op jit(solution)/shard_map/ppermute | solution.py:866
  81.5 14.7 %collective-permute-start.11 = (bf16[256,512]{1,0:T(8,128)(2,1)S(1)}, bf16[256,512]{1,0:T(8,128)(2,1)S(1)}, u32[]{:S(2)}, u32[]{:S(2)}) collective-permute-start(bf16[256,512]{1,0:T(8,128)(2,1)S(1)} %get-tuple-element.256), channel_id=1, source_target_pairs={{0,4},{1,5},{2,6},{3,7},{4,0},{5,1},{6,2},{7,3},{8,12},{9,13},{10,... | collective-permute-start | bytes 786440 | tf_op jit(solution)/shard_map/ppermute | solution.py:866
  83.1 13.1 %collective-permute-start.12 = (bf16[256,512]{1,0:T(8,128)(2,1)S(1)}, bf16[256,512]{1,0:T(8,128)(2,1)S(1)}, u32[]{:S(2)}, u32[]{:S(2)}) collective-permute-start(bf16[256,512]{1,0:T(8,128)(2,1)S(1)} %get-tuple-element.257), channel_id=1, source_target_pairs={{0,2},{1,3},{2,0},{3,1},{4,6},{5,7},{6,4},{7,5},{8,10},{9,11},{10,... | collective-permute-start | bytes 786440 | tf_op jit(solution)/shard_map/ppermute | solution.py:866
  83.6 10.7 %copy-start.12 = (bf16[1024,512]{1,0:T(8,128)(2,1)S(1)}, bf16[1024,512]{1,0:T(8,128)(2,1)}, u32[]{:S(2)}) copy-start(bf16[1024,512]{1,0:T(8,128)(2,1)} %get-tuple-element.250.h_ref) | copy-start | bytes 3145732
  96.6 8.2 %collective-permute-start.14 = (bf16[768,512]{1,0:T(8,128)(2,1)S(1)}, bf16[768,512]{1,0:T(8,128)(2,1)S(1)}, u32[]{:S(2)}, u32[]{:S(2)}) collective-permute-start(bf16[768,512]{1,0:T(8,128)(2,1)S(1)} %get-tuple-element.285), channel_id=1, source_target_pairs={{0,1},{1,0},{2,3},{3,2},{4,5},{5,4},{6,7},{7,6},{8,9},{9,8},{10,11... | collective-permute-start | bytes 2359304 | tf_op jit(solution)/shard_map/ppermute | solution.py:866
  96.7 17.1 %collective-permute-start.19 = (bf16[640,512]{1,0:T(8,128)(2,1)S(1)}, bf16[640,512]{1,0:T(8,128)(2,1)S(1)}, u32[]{:S(2)}, u32[]{:S(2)}) collective-permute-start(bf16[640,512]{1,0:T(8,128)(2,1)S(1)} %get-tuple-element.297), channel_id=1, source_target_pairs={{0,2},{1,3},{2,0},{3,1},{4,6},{5,7},{6,4},{7,5},{8,10},{9,11},{10,... | collective-permute-start | bytes 1966088 | tf_op jit(solution)/shard_map/ppermute | solution.py:866
  98.3 14.0 %collective-permute-start.18 = (bf16[512,512]{1,0:T(8,128)(2,1)S(1)}, bf16[512,512]{1,0:T(8,128)(2,1)S(1)}, u32[]{:S(2)}, u32[]{:S(2)}) collective-permute-start(bf16[512,512]{1,0:T(8,128)(2,1)S(1)} %get-tuple-element.296), channel_id=1, source_target_pairs={{0,4},{1,5},{2,6},{3,7},{4,0},{5,1},{6,2},{7,3},{8,12},{9,13},{10,... | collective-permute-start | bytes 1572872 | tf_op jit(solution)/shard_map/ppermute | solution.py:866
  98.7 8.1 %collective-permute-start.13 = (bf16[256,512]{1,0:T(8,128)(2,1)S(1)}, bf16[256,512]{1,0:T(8,128)(2,1)S(1)}, u32[]{:S(2)}, u32[]{:S(2)}) collective-permute-start(bf16[256,512]{1,0:T(8,128)(2,1)S(1)} %get-tuple-element.283), channel_id=1, source_target_pairs={{0,16},{16,0},{1,17},{17,1},{2,18},{18,2},{3,19},{19,3},{4,20},{20... | collective-permute-start | bytes 786440 | tf_op jit(solution)/shard_map/ppermute | solution.py:866
  103.6 1.2 collective-permute-start.15
  104.9 14.2 %collective-permute-start.17 = (bf16[416,512]{1,0:T(8,128)(2,1)S(1)}, bf16[416,512]{1,0:T(8,128)(2,1)S(1)}, u32[]{:S(2)}, u32[]{:S(2)}) collective-permute-start(bf16[416,512]{1,0:T(8,128)(2,1)S(1)} %get-tuple-element.289), channel_id=1, source_target_pairs={{0,16},{16,0},{1,17},{17,1},{2,18},{18,2},{3,19},{19,3},{4,20},{20... | collective-permute-start | bytes 1277960 | tf_op jit(solution)/shard_map/ppermute | solution.py:866
  114.0 12.7 %collective-permute-start.23 = (bf16[320,512]{1,0:T(8,128)(2,1)S(1)}, bf16[320,512]{1,0:T(8,128)(2,1)S(1)}, u32[]{:S(2)}, u32[]{:S(2)}) collective-permute-start(bf16[320,512]{1,0:T(8,128)(2,1)S(1)} %get-tuple-element.306), channel_id=1, source_target_pairs={{0,16},{16,0},{1,17},{17,1},{2,18},{18,2},{3,19},{19,3},{4,20},{20... | collective-permute-start | bytes 983048 | tf_op jit(solution)/shard_map/ppermute | solution.py:866
  114.6 12.1 %collective-permute-start.21 = (bf16[256,512]{1,0:T(8,128)(2,1)S(1)}, bf16[256,512]{1,0:T(8,128)(2,1)S(1)}, u32[]{:S(2)}, u32[]{:S(2)}) collective-permute-start(bf16[256,512]{1,0:T(8,128)(2,1)S(1)} %get-tuple-element.311), channel_id=1, source_target_pairs={{0,4},{1,5},{2,6},{3,7},{4,0},{5,1},{6,2},{7,3},{8,12},{9,13},{10,... | collective-permute-start | bytes 786440 | tf_op jit(solution)/shard_map/ppermute | solution.py:866
  114.9 11.8 %collective-permute-start.22 = (bf16[256,512]{1,0:T(8,128)(2,1)S(1)}, bf16[256,512]{1,0:T(8,128)(2,1)S(1)}, u32[]{:S(2)}, u32[]{:S(2)}) collective-permute-start(bf16[256,512]{1,0:T(8,128)(2,1)S(1)} %get-tuple-element.312), channel_id=1, source_target_pairs={{0,2},{1,3},{2,0},{3,1},{4,6},{5,7},{6,4},{7,5},{8,10},{9,11},{10,... | collective-permute-start | bytes 786440 | tf_op jit(solution)/shard_map/ppermute | solution.py:866
  116.6 7.9 %collective-permute-start.16 = (bf16[128,512]{1,0:T(8,128)(2,1)S(1)}, bf16[128,512]{1,0:T(8,128)(2,1)S(1)}, u32[]{:S(2)}, u32[]{:S(2)}) collective-permute-start(bf16[128,512]{1,0:T(8,128)(2,1)S(1)} %get-tuple-element.292), channel_id=1, source_target_pairs={{0,8},{1,9},{2,10},{3,11},{4,12},{5,13},{6,14},{7,15},{8,0},{9,1},... | collective-permute-start | bytes 393224 | tf_op jit(solution)/shard_map/ppermute | solution.py:866
  119.2 12.9 %collective-permute-start.27 = (bf16[224,512]{1,0:T(8,128)(2,1)S(1)}, bf16[224,512]{1,0:T(8,128)(2,1)S(1)}, u32[]{:S(2)}, u32[]{:S(2)}) collective-permute-start(bf16[224,512]{1,0:T(8,128)(2,1)S(1)} %get-tuple-element.308), channel_id=1, source_target_pairs={{0,4},{1,5},{2,6},{3,7},{4,0},{5,1},{6,2},{7,3},{8,12},{9,13},{10,... | collective-permute-start | bytes 688136 | tf_op jit(solution)/shard_map/ppermute | solution.py:866
  126.8 9.7 %collective-permute-start.26 = (bf16[160,512]{1,0:T(8,128)(2,1)S(1)}, bf16[160,512]{1,0:T(8,128)(2,1)S(1)}, u32[]{:S(2)}, u32[]{:S(2)}) collective-permute-start(bf16[160,512]{1,0:T(8,128)(2,1)S(1)} %get-tuple-element.324), channel_id=1, source_target_pairs={{0,8},{1,9},{2,10},{3,11},{4,12},{5,13},{6,14},{7,15},{8,0},{9,1},... | collective-permute-start | bytes 491528 | tf_op jit(solution)/shard_map/ppermute | solution.py:866
  128.1 5.7 %collective-permute-start.24 = (bf16[128,512]{1,0:T(8,128)(2,1)S(1)}, bf16[128,512]{1,0:T(8,128)(2,1)S(1)}, u32[]{:S(2)}, u32[]{:S(2)}) collective-permute-start(bf16[128,512]{1,0:T(8,128)(2,1)S(1)} %get-tuple-element.322), channel_id=1, source_target_pairs={{0,2},{1,3},{2,0},{3,1},{4,6},{5,7},{6,4},{7,5},{8,10},{9,11},{10,... | collective-permute-start | bytes 393224 | tf_op jit(solution)/shard_map/ppermute | solution.py:866
  129.7 5.0 %collective-permute-start.25 = (bf16[128,512]{1,0:T(8,128)(2,1)S(1)}, bf16[128,512]{1,0:T(8,128)(2,1)S(1)}, u32[]{:S(2)}, u32[]{:S(2)}) collective-permute-start(bf16[128,512]{1,0:T(8,128)(2,1)S(1)} %get-tuple-element.323), channel_id=1, source_target_pairs={{0,16},{16,0},{1,17},{17,1},{2,18},{18,2},{3,19},{19,3},{4,20},{20... | collective-permute-start | bytes 393224 | tf_op jit(solution)/shard_map/ppermute | solution.py:866
  132.1 6.9 %collective-permute-start.30 = (bf16[128,512]{1,0:T(8,128)(2,1)S(1)}, bf16[128,512]{1,0:T(8,128)(2,1)S(1)}, u32[]{:S(2)}, u32[]{:S(2)}) collective-permute-start(bf16[128,512]{1,0:T(8,128)(2,1)S(1)} %get-tuple-element.327), channel_id=1, source_target_pairs={{0,2},{1,3},{2,0},{3,1},{4,6},{5,7},{6,4},{7,5},{8,10},{9,11},{10,... | collective-permute-start | bytes 393224 | tf_op jit(solution)/shard_map/ppermute | solution.py:866
  136.6 8.1 %collective-permute-start.28 = (bf16[128,512]{1,0:T(8,128)(2,1)S(1)}, bf16[128,512]{1,0:T(8,128)(2,1)S(1)}, u32[]{:S(2)}, u32[]{:S(2)}) collective-permute-start(bf16[128,512]{1,0:T(8,128)(2,1)S(1)} %get-tuple-element.336), channel_id=1, source_target_pairs={{0,8},{1,9},{2,10},{3,11},{4,12},{5,13},{6,14},{7,15},{8,0},{9,1},... | collective-permute-start | bytes 393224 | tf_op jit(solution)/shard_map/ppermute | solution.py:866
  136.7 4.8 %collective-permute-start.29 = (bf16[80,512]{1,0:T(8,128)(2,1)S(1)}, bf16[80,512]{1,0:T(8,128)(2,1)S(1)}, u32[]{:S(2)}, u32[]{:S(2)}) collective-permute-start(bf16[80,512]{1,0:T(8,128)(2,1)S(1)} %get-tuple-element.337), channel_id=1, source_target_pairs={{0,4},{1,5},{2,6},{3,7},{4,0},{5,1},{6,2},{7,3},{8,12},{9,13},{10,... | collective-permute-start | bytes 245768 | tf_op jit(solution)/shard_map/ppermute | solution.py:866
  139.0 7.8 %collective-permute-start.33 = (bf16[80,512]{1,0:T(8,128)(2,1)S(1)}, bf16[80,512]{1,0:T(8,128)(2,1)S(1)}, u32[]{:S(2)}, u32[]{:S(2)}) collective-permute-start(bf16[80,512]{1,0:T(8,128)(2,1)S(1)} %get-tuple-element.340), channel_id=1, source_target_pairs={{0,8},{1,9},{2,10},{3,11},{4,12},{5,13},{6,14},{7,15},{8,0},{9,1},... | collective-permute-start | bytes 245768 | tf_op jit(solution)/shard_map/ppermute | solution.py:866
  139.7 7.6 %collective-permute-start.20 = (bf16[128,512]{1,0:T(8,128)(2,1)S(1)}, bf16[128,512]{1,0:T(8,128)(2,1)S(1)}, u32[]{:S(2)}, u32[]{:S(2)}) collective-permute-start(bf16[128,512]{1,0:T(8,128)(2,1)S(1)} %shard_map.208.refs_0_), channel_id=1, source_target_pairs={{0,16},{16,0},{1,17},{17,1},{2,18},{18,2},{3,19},{19,3},{4,20},{20... | collective-permute-start | bytes 393224 | tf_op jit(solution)/shard_map/ppermute | solution.py:866
  144.7 5.9 %collective-permute-start.31 = (bf16[128,512]{1,0:T(8,128)(2,1)S(1)}, bf16[128,512]{1,0:T(8,128)(2,1)S(1)}, u32[]{:S(2)}, u32[]{:S(2)}) collective-permute-start(bf16[128,512]{1,0:T(8,128)(2,1)S(1)} %shard_map.215.refs_2_), channel_id=1, source_target_pairs={{0,16},{16,0},{1,17},{17,1},{2,18},{18,2},{3,19},{19,3},{4,20},{20... | collective-permute-start | bytes 393224 | tf_op jit(solution)/shard_map/ppermute | solution.py:866
  145.2 5.5 %collective-permute-start.32 = (bf16[80,512]{1,0:T(8,128)(2,1)S(1)}, bf16[80,512]{1,0:T(8,128)(2,1)S(1)}, u32[]{:S(2)}, u32[]{:S(2)}) collective-permute-start(bf16[80,512]{1,0:T(8,128)(2,1)S(1)} %shard_map.216.refs_4_), channel_id=1, source_target_pairs={{0,16},{16,0},{1,17},{17,1},{2,18},{18,2},{3,19},{19,3},{4,20},{20... | collective-permute-start | bytes 245768 | tf_op jit(solution)/shard_map/ppermute | solution.py:866
  146.8 4.7 %collective-permute-start.34 = (bf16[80,512]{1,0:T(8,128)(2,1)S(1)}, bf16[80,512]{1,0:T(8,128)(2,1)S(1)}, u32[]{:S(2)}, u32[]{:S(2)}) collective-permute-start(bf16[80,512]{1,0:T(8,128)(2,1)S(1)} %shard_map.217.refs_6_), channel_id=1, source_target_pairs={{0,16},{16,0},{1,17},{17,1},{2,18},{18,2},{3,19},{19,3},{4,20},{20... | collective-permute-start | bytes 245768 | tf_op jit(solution)/shard_map/ppermute | solution.py:866
  (1 other events, 3.1 us)

commit v2 on v1

--- a/solution.py
+++ b/solution.py
@@ -460,7 +460,7 @@
     rows = 256
     gain = params_ref[1:2, 0:TILE]
 
-    @pl.loop(0, gr_ref.shape[0] // rows)
+    @pl.loop(0, gr_ref.shape[0] // rows, unroll=2)
     def _(f):
         span = rows_at(f, rows)
         grad_low = gr_ref[span, :]

time: 153 us -> 153 us (level)
  transfers between devices with their start and end apart: 35 -> 35, of which waited for: 15 -> 15; matrix products, arithmetic and copies ran while one was open for 1% -> 1% of each run, Pallas kernels for 40% -> 39%
where the time goes in v2:
time: 153 us
  Pallas kernels  88 us (58%)
  starting transfers between devices  34.5 us (23%)
  waiting for transfers between devices  28.4 us (19%)
    pallas_call x33, Pallas kernels, call(): pl.pallas_call(kernel, in_specs=[VMEM] * len(args) if specs is None else...  88 us
    ppermute x35, starting transfers between devices, swap(): return lax.ppermute(array, axis, [(i, i ^ 1 << bit) for i in range(size)])  34.5 us
    ppermute x35, waiting for transfers between devices, swap(): return lax.ppermute(array, axis, [(i, i ^ 1 << bit) for i in range(size)])  28.4 us
  transfers between devices with their start and end apart: 35, of which 15 were waited for; matrix products, arithmetic and copies ran while one was open for 1% of the time, Pallas kernels for 39%

profile of v2, /device:TPU:0, one launch (start us, length us, event | category | flops | bytes accessed | tf_op | source)
XLA Modules:
  0.0 153.1 jit_solution(1756154815592289653)
XLA Ops:
  0.6 0.5 collective-permute-start.1
  1.2 0.8 select_maximum_fusion.params_ref
  2.0 20.9 %shard_map.186 = (bf16[4,128,512]{2,1,0:T(8,128)(2,1)S(1)}, bf16[4,128,512]{2,1,0:T(8,128)(2,1)S(1)}, bf16[1024,512]{1,0:T(8,128)(2,1)}, bf16[1024,1536]{1,0:T(8...) custom-call(bf16[4,256,512]{2,1,0:T(8,128)(2,1)} %tok_ref.1, ...), custom_call_target="tpu_custom_call" | custom-call | flops 368000000 | tf_op jit(solution)/shard_map/pallas_call | solution.py:854
  23.0 1.9 %collective-permute-done.recv_ref = bf16[4,128,512]{2,1,0:T(8,128)(2,1)S(1)} collective-permute-done((bf16[4,128,512]{2,1,0:T(8,128)(2,1)S(1)}, bf16[4,128,512]{2,1,0:T(8,128)(2,1)S(1)}, u32[]{:S(2)}, u32[]{:S(2)}) %collective-permute-start) | collective-permute-done | bytes 524320 | tf_op jit(solution)/shard_map/ppermute | solution.py:866
  24.9 21.2 %shard_map.187 = (bf16[4,128,512]{2,1,0:T(8,128)(2,1)S(1)}, bf16[4,128,512]{2,1,0:T(8,128)(2,1)S(1)}, bf16[1024,512]{1,0:T(8,128)(2,1)S(1)}, bf16[1024,512]{1,0:...) custom-call(s32[8,8]{1,0:T(8,128)S(1)} %copy-done.13, ...), custom_call_target="tpu_custom_call" | custom-call | flops 552000000 | tf_op jit(solution)/shard_map/pallas_call | solution.py:854
  46.0 4.6 %shard_map.188 = (bf16[2048,512]{1,0:T(8,128)(2,1)S(1)}, bf16[2048,512]{1,0:T(8,128)(2,1)S(1)}) custom-call(bf16[1024,512]{1,0:T(8,128)(2,1)S(1)} %get-tuple-element.188.h_ref, bf16[1024,2048]{1,0:T(8,128)(2,1)S(1)} %get-tuple-element.189.du_ref, bf16[1024,2048]{1,0:T(8,128)(2,1)S(1)} %get-tuple-element.190.act_ref, ...), custom_call_target="tpu_custom_call" | custom-call | flops 103500000 | tf_op jit(solution)/shard_map/pallas_call | solution.py:854
  51.2 8.0 %shard_map.189 = (bf16[4,128,512]{2,1,0:T(8,128)(2,1)S(1)}, bf16[4,128,512]{2,1,0:T(8,128)(2,1)S(1)}, bf16[1024,512]{1,0:T(8,128)(2,1)S(1)}, bf16[1024,1536]{1,0:T(8,128)(2,1)S(1)}, f32[8,512]{1,0:T(8,128)S(1)}) custom-call(s32[8,8]{1,0:T(8,128)S(1)} %copy-done.13, bf16[1024,512]{1,0:T(8,128)(2,1)S(1)} %get-tuple-element.186.x_ref, ...), custom_call_target="tpu_custom_call" | custom-call | flops 184000000 | tf_op jit(solution)/shard_map/pallas_call | solution.py:854
  59.4 2.4 %shard_map.190 = (bf16[1024,512]{1,0:T(8,128)(2,1)S(1)}, bf16[1024,512]{1,0:T(8,128)(2,1)S(1)}) custom-call(bf16[1024,512]{1,0:T(8,128)(2,1)S(1)} %get-tuple-element.200.h_ref, bf16[1024,1536]{1,0:T(8,128)(2,1)S(1)} %get-tuple-element.201.dqkv_ref, bf16[1024,512]{1,0:T(8,128)(2,1)S(1)} %get-tuple-element.202.o_ref, ...), custom_call_target="tpu_custom_call" | custom-call | flops 55200000 | tf_op jit(solution)/shard_map/pallas_call | solution.py:854
  62.6 2.6 %collective-permute-start.5 = (bf16[512,512]{1,0:T(8,128)(2,1)S(1)}, bf16[512,512]{1,0:T(8,128)(2,1)S(1)}, u32[]{:S(2)}, u32[]{:S(2)}) collective-permute-start(bf16[512,512]{1,0:T(8,128)(2,1)S(1)} %get-tuple-element.230), channel_id=1, source_target_pairs={{0,2},{1,3},{2,0},{3,1},{4,6},{5,7},{6,4},{7,5},{8,10},{9,11},{10,... | collective-permute-start | bytes 1572872 | tf_op jit(solution)/shard_map/ppermute | solution.py:866
  65.2 1.6 %collective-permute-start.6 = (bf16[512,512]{1,0:T(8,128)(2,1)S(1)}, bf16[512,512]{1,0:T(8,128)(2,1)S(1)}, u32[]{:S(2)}, u32[]{:S(2)}) collective-permute-start(bf16[512,512]{1,0:T(8,128)(2,1)S(1)} %get-tuple-element.231), channel_id=1, source_target_pairs={{0,4},{1,5},{2,6},{3,7},{4,0},{5,1},{6,2},{7,3},{8,12},{9,13},{10,... | collective-permute-start | bytes 1572872 | tf_op jit(solution)/shard_map/ppermute | solution.py:866
  66.8 2.4 %shard_map.192 = (bf16[1024,512]{1,0:T(8,128)(2,1)S(1)}, bf16[1024,512]{1,0:T(8,128)(2,1)S(1)}, bf16[1024,512]{1,0:T(8,128)(2,1)S(1)}) custom-call(bf16[1024,2048]{1,0:T(8,128)(2,1)S(1)} %copy-done.5, bf16[4,128,512]{2,1,0:T(8,128)(2,1)S(1)} %get-tuple-element.217.own_ref, bf16[4,128,512]{2,1,0:T(8,128)(2,1)S(1)} %collective-permute-done.2.recv_ref), custom_call_target="tpu_custom_call" | custom-call | flops 55200000 | tf_op jit(solution)/shard_map/pallas_call | solution.py:854
  69.3 5.9 %shard_map.193 = (bf16[1024,2048]{1,0:T(8,128)(2,1)S(1)}, f32[1024,512]{1,0:T(8,128)S(1)}, bf16[1024,512]{1,0:T(8,128)(2,1)S(1)}, f32[8,512]{1,0:T(8,128)S(1)}) custom-call(bf16[1024,512]{1,0:T(8,128)(2,1)S(1)} %get-tuple-element.222.gr_ref, f32[1024,512]{1,0:T(8,128)S(1)} %copy-done.9, bf16[1024,2048]{1,0:T(8,128)(2,1)S(1)} %copy-done.6, ...), custom_call_target="tpu_custom_call" | custom-call | flops 138000000 | tf_op jit(solution)/shard_map/pallas_call | solution.py:854
  75.2 2.9 %shard_map.194 = (bf16[1280,512]{1,0:T(8,128)(2,1)S(1)}, bf16[1280,512]{1,0:T(8,128)(2,1)S(1)}) custom-call(bf16[1024,512]{1,0:T(8,128)(2,1)S(1)} %copy-done.11, bf16[1024,2048]{1,0:T(8,128)(2,1)S(1)} %get-tuple-element.225.du_ref, bf16[1024,512]{1,0:T(8,128)(2,1)S(1)} %copy-done.4, bf16[1024,512]{1,0:T(8,128)(2,1)S(1)} %get-tuple-element.247.ar_ref), custom_call_target="tpu_custom_call" | custom-call | flops 69000000 | tf_op jit(solution)/shard_map/pallas_call | solution.py:854
  78.1 1.0 collective-permute-done.6.refs_3_
  79.5 0.5 collective-permute-start.10
  80.0 1.5 %collective-permute-start.8 = (bf16[512,512]{1,0:T(8,128)(2,1)S(1)}, bf16[512,512]{1,0:T(8,128)(2,1)S(1)}, u32[]{:S(2)}, u32[]{:S(2)}) collective-permute-start(bf16[512,512]{1,0:T(8,128)(2,1)S(1)} %get-tuple-element.253), channel_id=1, source_target_pairs={{0,16},{16,0},{1,17},{17,1},{2,18},{18,2},{3,19},{19,3},{4,20},{20... | collective-permute-start | bytes 1572872 | tf_op jit(solution)/shard_map/ppermute | solution.py:866
  81.5 1.6 %collective-permute-start.11 = (bf16[256,512]{1,0:T(8,128)(2,1)S(1)}, bf16[256,512]{1,0:T(8,128)(2,1)S(1)}, u32[]{:S(2)}, u32[]{:S(2)}) collective-permute-start(bf16[256,512]{1,0:T(8,128)(2,1)S(1)} %get-tuple-element.256), channel_id=1, source_target_pairs={{0,4},{1,5},{2,6},{3,7},{4,0},{5,1},{6,2},{7,3},{8,12},{9,13},{10,... | collective-permute-start | bytes 786440 | tf_op jit(solution)/shard_map/ppermute | solution.py:866
  83.1 0.5 collective-permute-start.12
  83.6 10.7 %shard_map.197.dqkv_ref = bf16[1024,1536]{1,0:T(8,128)(2,1)S(1)} custom-call(bf16[1024,512]{1,0:T(8,128)(2,1)S(1)} %get-tuple-element.247.ar_ref, bf16[1024,1536]{1,0:T(8,128)(2,1)S(1)} %copy-done.8, f32[4,8,256]{2,1,0:T(8,128)S(1)} %get-tuple-element.249.lse_ref, bf16[1024,512]{1,0:T(8,128)(2,1)S(1)} %copy-done.4, bf16[2,512,512]{2,1,0:T(8,128)(2,1)S(1)} %copy-done.3), custom_call_target="tpu_custom_call" | custom-call | flops 230000000 | tf_op jit(solution)/shard_map/pallas_call | solution.py:854
  94.3 1.8 %shard_map.198 = (bf16[768,512]{1,0:T(8,128)(2,1)S(1)}, bf16[768,512]{1,0:T(8,128)(2,1)S(1)}) custom-call(bf16[1024,1536]{1,0:T(8,128)(2,1)S(1)} %shard_map.197.dqkv_ref, bf16[1024,512]{1,0:T(8,128)(2,1)S(1)} %copy-done.12), custom_call_target="tpu_custom_call" | custom-call | flops 46000000 | tf_op jit(solution)/shard_map/pallas_call | solution.py:854
  96.7 1.6 %collective-permute-start.19 = (bf16[640,512]{1,0:T(8,128)(2,1)S(1)}, bf16[640,512]{1,0:T(8,128)(2,1)S(1)}, u32[]{:S(2)}, u32[]{:S(2)}) collective-permute-start(bf16[640,512]{1,0:T(8,128)(2,1)S(1)} %get-tuple-element.297), channel_id=1, source_target_pairs={{0,2},{1,3},{2,0},{3,1},{4,6},{5,7},{6,4},{7,5},{8,10},{9,11},{10,... | collective-permute-start | bytes 1966088 | tf_op jit(solution)/shard_map/ppermute | solution.py:866
  98.7 0.5 collective-permute-start.13
  99.2 4.4 %shard_map.202 = (bf16[4,256,512]{2,1,0:T(8,128)(2,1)}, bf16[4,256,512]{2,1,0:T(8,128)(2,1)}, bf16[32,512]{1,0:T(8,128)(2,1)S(1)}) custom-call(bf16[1024,1536]{1,0:T(8,128)(2,1)S(1)} %shard_map.197.dqkv_ref, bf16[4,256,512]{2,1,0:T(8,128)(2,1)S(1)} %copy-done.7, f32[1024,512]{1,0:T(8,128)S(1)} %get-tuple-element.274.dxa_ref, ...), custom_call_target="tpu_custom_call" | custom-call | flops 92000000 | tf_op jit(solution)/shard_map/pallas_call | solution.py:854
  103.6 1.2 collective-permute-done.15.refs_3_
  104.9 1.6 %collective-permute-start.17 = (bf16[416,512]{1,0:T(8,128)(2,1)S(1)}, bf16[416,512]{1,0:T(8,128)(2,1)S(1)}, u32[]{:S(2)}, u32[]{:S(2)}) collective-permute-start(bf16[416,512]{1,0:T(8,128)(2,1)S(1)} %get-tuple-element.289), channel_id=1, source_target_pairs={{0,16},{16,0},{1,17},{17,1},{2,18},{18,2},{3,19},{19,3},{4,20},{20... | collective-permute-start | bytes 1277960 | tf_op jit(solution)/shard_map/ppermute | solution.py:866
  106.9 5.4 %collective-permute-done.18.refs_3_ = bf16[512,512]{1,0:T(8,128)(2,1)S(1)} collective-permute-done((bf16[512,512]{1,0:T(8,128)(2,1)S(1)}, bf16[512,512]{1,0:T(8,128)(2,1)S(1)}, u32[]{:S(2)}, u32[]{:S(2)}) %collective-permute-start.18) | collective-permute-done | bytes 524320 | tf_op jit(solution)/shard_map/ppermute | solution.py:866
  112.3 1.6 %collective-permute-done.19.refs_1_ = bf16[640,512]{1,0:T(8,128)(2,1)S(1)} collective-permute-done((bf16[640,512]{1,0:T(8,128)(2,1)S(1)}, bf16[640,512]{1,0:T(8,128)(2,1)S(1)}, u32[]{:S(2)}, u32[]{:S(2)}) %collective-permute-start.19) | collective-permute-done | bytes 655392 | tf_op jit(solution)/shard_map/ppermute | solution.py:866
  114.0 0.6 collective-permute-start.23
  114.9 1.7 %collective-permute-start.22 = (bf16[256,512]{1,0:T(8,128)(2,1)S(1)}, bf16[256,512]{1,0:T(8,128)(2,1)S(1)}, u32[]{:S(2)}, u32[]{:S(2)}) collective-permute-start(bf16[256,512]{1,0:T(8,128)(2,1)S(1)} %get-tuple-element.312), channel_id=1, source_target_pairs={{0,2},{1,3},{2,0},{3,1},{4,6},{5,7},{6,4},{7,5},{8,10},{9,11},{10,... | collective-permute-start | bytes 786440 | tf_op jit(solution)/shard_map/ppermute | solution.py:866
  116.6 2.6 %collective-permute-start.16 = (bf16[128,512]{1,0:T(8,128)(2,1)S(1)}, bf16[128,512]{1,0:T(8,128)(2,1)S(1)}, u32[]{:S(2)}, u32[]{:S(2)}) collective-permute-start(bf16[128,512]{1,0:T(8,128)(2,1)S(1)} %get-tuple-element.292), channel_id=1, source_target_pairs={{0,8},{1,9},{2,10},{3,11},{4,12},{5,13},{6,14},{7,15},{8,0},{9,1},... | collective-permute-start | bytes 393224 | tf_op jit(solution)/shard_map/ppermute | solution.py:866
  119.2 1.7 %collective-permute-start.27 = (bf16[224,512]{1,0:T(8,128)(2,1)S(1)}, bf16[224,512]{1,0:T(8,128)(2,1)S(1)}, u32[]{:S(2)}, u32[]{:S(2)}) collective-permute-start(bf16[224,512]{1,0:T(8,128)(2,1)S(1)} %get-tuple-element.308), channel_id=1, source_target_pairs={{0,4},{1,5},{2,6},{3,7},{4,0},{5,1},{6,2},{7,3},{8,12},{9,13},{10,... | collective-permute-start | bytes 688136 | tf_op jit(solution)/shard_map/ppermute | solution.py:866
  120.9 3.6 %collective-permute-done.16.refs_1_ = bf16[128,512]{1,0:T(8,128)(2,1)S(1)} collective-permute-done((bf16[128,512]{1,0:T(8,128)(2,1)S(1)}, bf16[128,512]{1,0:T(8,128)(2,1)S(1)}, u32[]{:S(2)}, u32[]{:S(2)}) %collective-permute-start.16) | collective-permute-done | bytes 131104 | tf_op jit(solution)/shard_map/ppermute | solution.py:866
  124.5 2.2 %collective-permute-done.21.refs_1_ = bf16[256,512]{1,0:T(8,128)(2,1)S(1)} collective-permute-done((bf16[256,512]{1,0:T(8,128)(2,1)S(1)}, bf16[256,512]{1,0:T(8,128)(2,1)S(1)}, u32[]{:S(2)}, u32[]{:S(2)}) %collective-permute-start.21) | collective-permute-done | bytes 262176 | tf_op jit(solution)/shard_map/ppermute | solution.py:866
  126.8 1.3 collective-permute-start.26
  128.1 1.7 %collective-permute-start.24 = (bf16[128,512]{1,0:T(8,128)(2,1)S(1)}, bf16[128,512]{1,0:T(8,128)(2,1)S(1)}, u32[]{:S(2)}, u32[]{:S(2)}) collective-permute-start(bf16[128,512]{1,0:T(8,128)(2,1)S(1)} %get-tuple-element.322), channel_id=1, source_target_pairs={{0,2},{1,3},{2,0},{3,1},{4,6},{5,7},{6,4},{7,5},{8,10},{9,11},{10,... | collective-permute-start | bytes 393224 | tf_op jit(solution)/shard_map/ppermute | solution.py:866
  129.7 1.5 %collective-permute-start.25 = (bf16[128,512]{1,0:T(8,128)(2,1)S(1)}, bf16[128,512]{1,0:T(8,128)(2,1)S(1)}, u32[]{:S(2)}, u32[]{:S(2)}) collective-permute-start(bf16[128,512]{1,0:T(8,128)(2,1)S(1)} %get-tuple-element.323), channel_id=1, source_target_pairs={{0,16},{16,0},{1,17},{17,1},{2,18},{18,2},{3,19},{19,3},{4,20},{20... | collective-permute-start | bytes 393224 | tf_op jit(solution)/shard_map/ppermute | solution.py:866
  131.3 0.8 collective-permute-done.27.refs_1_
  132.1 1.7 %collective-permute-start.30 = (bf16[128,512]{1,0:T(8,128)(2,1)S(1)}, bf16[128,512]{1,0:T(8,128)(2,1)S(1)}, u32[]{:S(2)}, u32[]{:S(2)}) collective-permute-start(bf16[128,512]{1,0:T(8,128)(2,1)S(1)} %get-tuple-element.327), channel_id=1, source_target_pairs={{0,2},{1,3},{2,0},{3,1},{4,6},{5,7},{6,4},{7,5},{8,10},{9,11},{10,... | collective-permute-start | bytes 393224 | tf_op jit(solution)/shard_map/ppermute | solution.py:866
  133.8 0.9 collective-permute-done.25.refs_3_
  134.7 1.8 %collective-permute-done.26.refs_1_ = bf16[160,512]{1,0:T(8,128)(2,1)S(1)} collective-permute-done((bf16[160,512]{1,0:T(8,128)(2,1)S(1)}, bf16[160,512]{1,0:T(8,128)(2,1)S(1)}, u32[]{:S(2)}, u32[]{:S(2)}) %collective-permute-start.26) | collective-permute-done | bytes 163872 | tf_op jit(solution)/shard_map/ppermute | solution.py:866
  136.7 2.3 %collective-permute-start.29 = (bf16[80,512]{1,0:T(8,128)(2,1)S(1)}, bf16[80,512]{1,0:T(8,128)(2,1)S(1)}, u32[]{:S(2)}, u32[]{:S(2)}) collective-permute-start(bf16[80,512]{1,0:T(8,128)(2,1)S(1)} %get-tuple-element.337), channel_id=1, source_target_pairs={{0,4},{1,5},{2,6},{3,7},{4,0},{5,1},{6,2},{7,3},{8,12},{9,13},{10,... | collective-permute-start | bytes 245768 | tf_op jit(solution)/shard_map/ppermute | solution.py:866
  139.0 0.6 collective-permute-start.33
  139.7 1.6 %collective-permute-start.20 = (bf16[128,512]{1,0:T(8,128)(2,1)S(1)}, bf16[128,512]{1,0:T(8,128)(2,1)S(1)}, u32[]{:S(2)}, u32[]{:S(2)}) collective-permute-start(bf16[128,512]{1,0:T(8,128)(2,1)S(1)} %shard_map.208.refs_0_), channel_id=1, source_target_pairs={{0,16},{16,0},{1,17},{17,1},{2,18},{18,2},{3,19},{19,3},{4,20},{20... | collective-permute-start | bytes 393224 | tf_op jit(solution)/shard_map/ppermute | solution.py:866
  141.4 3.2 %collective-permute-done.28.refs_1_ = bf16[128,512]{1,0:T(8,128)(2,1)S(1)} collective-permute-done((bf16[128,512]{1,0:T(8,128)(2,1)S(1)}, bf16[128,512]{1,0:T(8,128)(2,1)S(1)}, u32[]{:S(2)}, u32[]{:S(2)}) %collective-permute-start.28) | collective-permute-done | bytes 131104 | tf_op jit(solution)/shard_map/ppermute | solution.py:866
  145.2 1.6 %collective-permute-start.32 = (bf16[80,512]{1,0:T(8,128)(2,1)S(1)}, bf16[80,512]{1,0:T(8,128)(2,1)S(1)}, u32[]{:S(2)}, u32[]{:S(2)}) collective-permute-start(bf16[80,512]{1,0:T(8,128)(2,1)S(1)} %shard_map.216.refs_4_), channel_id=1, source_target_pairs={{0,16},{16,0},{1,17},{17,1},{2,18},{18,2},{3,19},{19,3},{4,20},{20... | collective-permute-start | bytes 245768 | tf_op jit(solution)/shard_map/ppermute | solution.py:866
  147.3 3.4 %collective-permute-done.32.refs_5_ = bf16[80,512]{1,0:T(8,128)(2,1)S(1)} collective-permute-done((bf16[80,512]{1,0:T(8,128)(2,1)S(1)}, bf16[80,512]{1,0:T(8,128)(2,1)S(1)}, u32[]{:S(2)}, u32[]{:S(2)}) %collective-permute-start.32) | collective-permute-done | bytes 81952 | tf_op jit(solution)/shard_map/ppermute | solution.py:866
  150.6 0.9 collective-permute-done.34.refs_7_
  151.5 1.4 shard_map.218
  (84 shorter events, 5.3 us)
Async XLA Ops:
  0.6 24.2 %collective-permute-start.1 = (bf16[4,256,512]{2,1,0:T(8,128)(2,1)}, bf16[4,256,512]{2,1,0:T(8,128)(2,1)S(1)}, u32[]{:S(2)}, u32[]{:S(2)}) collective-permute-start(bf16[4,256,512]{2,1,0:T(8,128)(2,1)} %cot_ref.1), channel_id=1, source_target_pairs={{0,1},{1,0},{2,3},{3,2},{4,5},{5,4},{6,7},{7,6},{8,9},{9,8},{10,11... | collective-permute-start | bytes 3145736 | tf_op jit(solution)/shard_map/ppermute | solution.py:866
  1.9 22.9 %copy-start.2 = (bf16[2,512,1536]{2,1,0:T(8,128)(2,1)S(1)}, bf16[2,512,1536]{2,1,0:T(8,128)(2,1)}, u32[]{:S(2)}) copy-start(bf16[2,512,1536]{2,1,0:T(8,128)(2,1)} %wqkv_ref.1) | copy-start | bytes 9437188
  2.0 22.9 %copy-start.3 = (bf16[2,512,512]{2,1,0:T(8,128)(2,1)S(1)}, bf16[2,512,512]{2,1,0:T(8,128)(2,1)}, u32[]{:S(2)}) copy-start(bf16[2,512,512]{2,1,0:T(8,128)(2,1)} %wout_ref.1) | copy-start | bytes 3145732
  2.0 22.9 %copy-start.10 = (bf16[4,256,512]{2,1,0:T(8,128)(2,1)S(1)}, bf16[4,256,512]{2,1,0:T(8,128)(2,1)}, u32[]{:S(2)}) copy-start(bf16[4,256,512]{2,1,0:T(8,128)(2,1)} %cot_ref.1) | copy-start | bytes 3145732
  2.0 22.9 %copy-start.13 = (s32[8,8]{1,0:T(8,128)S(1)}, s32[8,8]{1,0:T(8,128)}, u32[]{:S(2)}) copy-start(s32[8,8]{1,0:T(8,128)} %slots_ref.3) | copy-start | bytes 772
  22.9 2.0 %collective-permute-start = (bf16[4,128,512]{2,1,0:T(8,128)(2,1)S(1)}, bf16[4,128,512]{2,1,0:T(8,128)(2,1)S(1)}, u32[]{:S(2)}, u32[]{:S(2)}) collective-permute-start(bf16[4,128,512]{2,1,0:T(8,128)(2,1)S(1)} %get-tuple-element.185), channel_id=1, source_target_pairs={{0,1},{1,0},{2,3},{3,2},{4,5},{5,4},{6,7},{7,6},{8,9},{9,8},{10,11... | collective-permute-start | bytes 1572872 | tf_op jit(solution)/shard_map/ppermute | solution.py:866
  50.6 11.2 %collective-permute-start.4 = (bf16[2048,512]{1,0:T(8,128)(2,1)S(1)}, bf16[2048,512]{1,0:T(8,128)(2,1)S(1)}, u32[]{:S(2)}, u32[]{:S(2)}) collective-permute-start(bf16[2048,512]{1,0:T(8,128)(2,1)S(1)} %get-tuple-element.207), channel_id=1, source_target_pairs={{0,1},{1,0},{2,3},{3,2},{4,5},{5,4},{6,7},{7,6},{8,9},{9,8},{10,11... | collective-permute-start | bytes 6291464 | tf_op jit(solution)/shard_map/ppermute | solution.py:866
  50.8 11.0 %collective-permute-start.3 = (bf16[4,128,512]{2,1,0:T(8,128)(2,1)S(1)}, bf16[4,128,512]{2,1,0:T(8,128)(2,1)S(1)}, u32[]{:S(2)}, u32[]{:S(2)}) collective-permute-start(bf16[4,128,512]{2,1,0:T(8,128)(2,1)S(1)} %get-tuple-element.206), channel_id=1, source_target_pairs={{0,1},{1,0},{2,3},{3,2},{4,5},{5,4},{6,7},{7,6},{8,9},{9,8},{10,11... | collective-permute-start | bytes 1572872 | tf_op jit(solution)/shard_map/ppermute | solution.py:866
  51.2 18.0 %copy-start.6 = (bf16[1024,2048]{1,0:T(8,128)(2,1)S(1)}, bf16[1024,2048]{1,0:T(8,128)(2,1)}, u32[]{:S(2)}) copy-start(bf16[1024,2048]{1,0:T(8,128)(2,1)} %get-tuple-element.224.slope_ref) | copy-start | bytes 12582916
  59.2 2.6 %collective-permute-start.2 = (bf16[4,128,512]{2,1,0:T(8,128)(2,1)S(1)}, bf16[4,128,512]{2,1,0:T(8,128)(2,1)S(1)}, u32[]{:S(2)}, u32[]{:S(2)}) collective-permute-start(bf16[4,128,512]{2,1,0:T(8,128)(2,1)S(1)} %get-tuple-element.199), channel_id=1, source_target_pairs={{0,1},{1,0},{2,3},{3,2},{4,5},{5,4},{6,7},{7,6},{8,9},{9,8},{10,11... | collective-permute-start | bytes 1572872 | tf_op jit(solution)/shard_map/ppermute | solution.py:866
  59.4 7.4 %copy-start.5 = (bf16[1024,2048]{1,0:T(8,128)(2,1)S(1)}, bf16[1024,2048]{1,0:T(8,128)(2,1)}, u32[]{:S(2)}) copy-start(bf16[1024,2048]{1,0:T(8,128)(2,1)} %get-tuple-element.183.act_ref) | copy-start | bytes 12582916
  59.4 9.8 %copy-start.9 = (f32[1024,512]{1,0:T(8,128)S(1)}, f32[1024,512]{1,0:T(8,128)}, u32[]{:S(2)}) copy-start(f32[1024,512]{1,0:T(8,128)} %get-tuple-element.223.xa_ref) | copy-start | bytes 6291460
  61.8 7.4 %copy-start.1 = (bf16[2,2048,512]{2,1,0:T(8,128)(2,1)S(1)}, bf16[2,2048,512]{2,1,0:T(8,128)(2,1)}, u32[]{:S(2)}) copy-start(bf16[2,2048,512]{2,1,0:T(8,128)(2,1)} %wdown_ref.1) | copy-start | bytes 12582916
  62.2 7.1 %copy-start = (bf16[2,512,2048]{2,1,0:T(8,128)(2,1)S(1)}, bf16[2,512,2048]{2,1,0:T(8,128)(2,1)}, u32[]{:S(2)}) copy-start(bf16[2,512,2048]{2,1,0:T(8,128)(2,1)} %wup_ref.1) | copy-start | bytes 12582916
  62.2 17.0 %collective-permute-start.7 = (bf16[1024,512]{1,0:T(8,128)(2,1)S(1)}, bf16[1024,512]{1,0:T(8,128)(2,1)S(1)}, u32[]{:S(2)}, u32[]{:S(2)}) collective-permute-start(bf16[1024,512]{1,0:T(8,128)(2,1)S(1)} %get-tuple-element.232), channel_id=1, source_target_pairs={{0,1},{1,0},{2,3},{3,2},{4,5},{5,4},{6,7},{7,6},{8,9},{9,8},{10,11... | collective-permute-start | bytes 3145736 | tf_op jit(solution)/shard_map/ppermute | solution.py:866
  62.6 15.5 %collective-permute-start.5 = (bf16[512,512]{1,0:T(8,128)(2,1)S(1)}, bf16[512,512]{1,0:T(8,128)(2,1)S(1)}, u32[]{:S(2)}, u32[]{:S(2)}) collective-permute-start(bf16[512,512]{1,0:T(8,128)(2,1)S(1)} %get-tuple-element.230), channel_id=1, source_target_pairs={{0,2},{1,3},{2,0},{3,1},{4,6},{5,7},{6,4},{7,5},{8,10},{9,11},{10,... | collective-permute-start | bytes 1572872 | tf_op jit(solution)/shard_map/ppermute | solution.py:866
  65.2 13.9 %collective-permute-start.6 = (bf16[512,512]{1,0:T(8,128)(2,1)S(1)}, bf16[512,512]{1,0:T(8,128)(2,1)S(1)}, u32[]{:S(2)}, u32[]{:S(2)}) collective-permute-start(bf16[512,512]{1,0:T(8,128)(2,1)S(1)} %get-tuple-element.231), channel_id=1, source_target_pairs={{0,4},{1,5},{2,6},{3,7},{4,0},{5,1},{6,2},{7,3},{8,12},{9,13},{10,... | collective-permute-start | bytes 1572872 | tf_op jit(solution)/shard_map/ppermute | solution.py:866
  69.3 5.9 %copy-start.4 = (bf16[1024,512]{1,0:T(8,128)(2,1)S(1)}, bf16[1024,512]{1,0:T(8,128)(2,1)}, u32[]{:S(2)}) copy-start(bf16[1024,512]{1,0:T(8,128)(2,1)} %get-tuple-element.226.o_ref) | copy-start | bytes 3145732
  69.3 5.9 %copy-start.11 = (bf16[1024,512]{1,0:T(8,128)(2,1)S(1)}, bf16[1024,512]{1,0:T(8,128)(2,1)}, u32[]{:S(2)}) copy-start(bf16[1024,512]{1,0:T(8,128)(2,1)} %get-tuple-element.221.h_ref) | copy-start | bytes 3145732
  78.1 5.5 %copy-start.8 = (bf16[1024,1536]{1,0:T(8,128)(2,1)S(1)}, bf16[1024,1536]{1,0:T(8,128)(2,1)}, u32[]{:S(2)}) copy-start(bf16[1024,1536]{1,0:T(8,128)(2,1)} %get-tuple-element.248.qkv_ref) | copy-start | bytes 9437188
  79.4 16.8 %collective-permute-start.9 = (bf16[1280,512]{1,0:T(8,128)(2,1)S(1)}, bf16[1280,512]{1,0:T(8,128)(2,1)S(1)}, u32[]{:S(2)}, u32[]{:S(2)}) collective-permute-start(bf16[1280,512]{1,0:T(8,128)(2,1)S(1)} %get-tuple-element.254), channel_id=1, source_target_pairs={{0,1},{1,0},{2,3},{3,2},{4,5},{5,4},{6,7},{7,6},{8,9},{9,8},{10,11... | collective-permute-start | bytes 3932168 | tf_op jit(solution)/shard_map/ppermute | solution.py:866
  79.5 16.7 %collective-permute-start.10 = (bf16[1024,512]{1,0:T(8,128)(2,1)S(1)}, bf16[1024,512]{1,0:T(8,128)(2,1)S(1)}, u32[]{:S(2)}, u32[]{:S(2)}) collective-permute-start(bf16[1024,512]{1,0:T(8,128)(2,1)S(1)} %get-tuple-element.255), channel_id=1, source_target_pairs={{0,1},{1,0},{2,3},{3,2},{4,5},{5,4},{6,7},{7,6},{8,9},{9,8},{10,11... | collective-permute-start | bytes 3145736 | tf_op jit(solution)/shard_map/ppermute | solution.py:866
  80.0 16.2 %collective-permute-start.8 = (bf16[512,512]{1,0:T(8,128)(2,1)S(1)}, bf16[512,512]{1,0:T(8,128)(2,1)S(1)}, u32[]{:S(2)}, u32[]{:S(2)}) collective-permute-start(bf16[512,512]{1,0:T(8,128)(2,1)S(1)} %get-tuple-element.253), channel_id=1, source_target_pairs={{0,16},{16,0},{1,17},{17,1},{2,18},{18,2},{3,19},{19,3},{4,20},{20... | collective-permute-start | bytes 1572872 | tf_op jit(solution)/shard_map/ppermute | solution.py:866
  81.5 14.7 %collective-permute-start.11 = (bf16[256,512]{1,0:T(8,128)(2,1)S(1)}, bf16[256,512]{1,0:T(8,128)(2,1)S(1)}, u32[]{:S(2)}, u32[]{:S(2)}) collective-permute-start(bf16[256,512]{1,0:T(8,128)(2,1)S(1)} %get-tuple-element.256), channel_id=1, source_target_pairs={{0,4},{1,5},{2,6},{3,7},{4,0},{5,1},{6,2},{7,3},{8,12},{9,13},{10,... | collective-permute-start | bytes 786440 | tf_op jit(solution)/shard_map/ppermute | solution.py:866
  83.1 13.1 %collective-permute-start.12 = (bf16[256,512]{1,0:T(8,128)(2,1)S(1)}, bf16[256,512]{1,0:T(8,128)(2,1)S(1)}, u32[]{:S(2)}, u32[]{:S(2)}) collective-permute-start(bf16[256,512]{1,0:T(8,128)(2,1)S(1)} %get-tuple-element.257), channel_id=1, source_target_pairs={{0,2},{1,3},{2,0},{3,1},{4,6},{5,7},{6,4},{7,5},{8,10},{9,11},{10,... | collective-permute-start | bytes 786440 | tf_op jit(solution)/shard_map/ppermute | solution.py:866
  83.6 10.7 %copy-start.12 = (bf16[1024,512]{1,0:T(8,128)(2,1)S(1)}, bf16[1024,512]{1,0:T(8,128)(2,1)}, u32[]{:S(2)}) copy-start(bf16[1024,512]{1,0:T(8,128)(2,1)} %get-tuple-element.250.h_ref) | copy-start | bytes 3145732
  96.6 8.2 %collective-permute-start.14 = (bf16[768,512]{1,0:T(8,128)(2,1)S(1)}, bf16[768,512]{1,0:T(8,128)(2,1)S(1)}, u32[]{:S(2)}, u32[]{:S(2)}) collective-permute-start(bf16[768,512]{1,0:T(8,128)(2,1)S(1)} %get-tuple-element.285), channel_id=1, source_target_pairs={{0,1},{1,0},{2,3},{3,2},{4,5},{5,4},{6,7},{7,6},{8,9},{9,8},{10,11... | collective-permute-start | bytes 2359304 | tf_op jit(solution)/shard_map/ppermute | solution.py:866
  96.7 17.1 %collective-permute-start.19 = (bf16[640,512]{1,0:T(8,128)(2,1)S(1)}, bf16[640,512]{1,0:T(8,128)(2,1)S(1)}, u32[]{:S(2)}, u32[]{:S(2)}) collective-permute-start(bf16[640,512]{1,0:T(8,128)(2,1)S(1)} %get-tuple-element.297), channel_id=1, source_target_pairs={{0,2},{1,3},{2,0},{3,1},{4,6},{5,7},{6,4},{7,5},{8,10},{9,11},{10,... | collective-permute-start | bytes 1966088 | tf_op jit(solution)/shard_map/ppermute | solution.py:866
  98.3 14.0 %collective-permute-start.18 = (bf16[512,512]{1,0:T(8,128)(2,1)S(1)}, bf16[512,512]{1,0:T(8,128)(2,1)S(1)}, u32[]{:S(2)}, u32[]{:S(2)}) collective-permute-start(bf16[512,512]{1,0:T(8,128)(2,1)S(1)} %get-tuple-element.296), channel_id=1, source_target_pairs={{0,4},{1,5},{2,6},{3,7},{4,0},{5,1},{6,2},{7,3},{8,12},{9,13},{10,... | collective-permute-start | bytes 1572872 | tf_op jit(solution)/shard_map/ppermute | solution.py:866
  98.7 8.1 %collective-permute-start.13 = (bf16[256,512]{1,0:T(8,128)(2,1)S(1)}, bf16[256,512]{1,0:T(8,128)(2,1)S(1)}, u32[]{:S(2)}, u32[]{:S(2)}) collective-permute-start(bf16[256,512]{1,0:T(8,128)(2,1)S(1)} %get-tuple-element.283), channel_id=1, source_target_pairs={{0,16},{16,0},{1,17},{17,1},{2,18},{18,2},{3,19},{19,3},{4,20},{20... | collective-permute-start | bytes 786440 | tf_op jit(solution)/shard_map/ppermute | solution.py:866
  103.6 1.2 collective-permute-start.15
  104.9 14.2 %collective-permute-start.17 = (bf16[416,512]{1,0:T(8,128)(2,1)S(1)}, bf16[416,512]{1,0:T(8,128)(2,1)S(1)}, u32[]{:S(2)}, u32[]{:S(2)}) collective-permute-start(bf16[416,512]{1,0:T(8,128)(2,1)S(1)} %get-tuple-element.289), channel_id=1, source_target_pairs={{0,16},{16,0},{1,17},{17,1},{2,18},{18,2},{3,19},{19,3},{4,20},{20... | collective-permute-start | bytes 1277960 | tf_op jit(solution)/shard_map/ppermute | solution.py:866
  114.0 12.7 %collective-permute-start.23 = (bf16[320,512]{1,0:T(8,128)(2,1)S(1)}, bf16[320,512]{1,0:T(8,128)(2,1)S(1)}, u32[]{:S(2)}, u32[]{:S(2)}) collective-permute-start(bf16[320,512]{1,0:T(8,128)(2,1)S(1)} %get-tuple-element.306), channel_id=1, source_target_pairs={{0,16},{16,0},{1,17},{17,1},{2,18},{18,2},{3,19},{19,3},{4,20},{20... | collective-permute-start | bytes 983048 | tf_op jit(solution)/shard_map/ppermute | solution.py:866
  114.6 12.1 %collective-permute-start.21 = (bf16[256,512]{1,0:T(8,128)(2,1)S(1)}, bf16[256,512]{1,0:T(8,128)(2,1)S(1)}, u32[]{:S(2)}, u32[]{:S(2)}) collective-permute-start(bf16[256,512]{1,0:T(8,128)(2,1)S(1)} %get-tuple-element.311), channel_id=1, source_target_pairs={{0,4},{1,5},{2,6},{3,7},{4,0},{5,1},{6,2},{7,3},{8,12},{9,13},{10,... | collective-permute-start | bytes 786440 | tf_op jit(solution)/shard_map/ppermute | solution.py:866
  114.9 11.8 %collective-permute-start.22 = (bf16[256,512]{1,0:T(8,128)(2,1)S(1)}, bf16[256,512]{1,0:T(8,128)(2,1)S(1)}, u32[]{:S(2)}, u32[]{:S(2)}) collective-permute-start(bf16[256,512]{1,0:T(8,128)(2,1)S(1)} %get-tuple-element.312), channel_id=1, source_target_pairs={{0,2},{1,3},{2,0},{3,1},{4,6},{5,7},{6,4},{7,5},{8,10},{9,11},{10,... | collective-permute-start | bytes 786440 | tf_op jit(solution)/shard_map/ppermute | solution.py:866
  116.6 7.9 %collective-permute-start.16 = (bf16[128,512]{1,0:T(8,128)(2,1)S(1)}, bf16[128,512]{1,0:T(8,128)(2,1)S(1)}, u32[]{:S(2)}, u32[]{:S(2)}) collective-permute-start(bf16[128,512]{1,0:T(8,128)(2,1)S(1)} %get-tuple-element.292), channel_id=1, source_target_pairs={{0,8},{1,9},{2,10},{3,11},{4,12},{5,13},{6,14},{7,15},{8,0},{9,1},... | collective-permute-start | bytes 393224 | tf_op jit(solution)/shard_map/ppermute | solution.py:866
  119.2 12.9 %collective-permute-start.27 = (bf16[224,512]{1,0:T(8,128)(2,1)S(1)}, bf16[224,512]{1,0:T(8,128)(2,1)S(1)}, u32[]{:S(2)}, u32[]{:S(2)}) collective-permute-start(bf16[224,512]{1,0:T(8,128)(2,1)S(1)} %get-tuple-element.308), channel_id=1, source_target_pairs={{0,4},{1,5},{2,6},{3,7},{4,0},{5,1},{6,2},{7,3},{8,12},{9,13},{10,... | collective-permute-start | bytes 688136 | tf_op jit(solution)/shard_map/ppermute | solution.py:866
  126.8 9.7 %collective-permute-start.26 = (bf16[160,512]{1,0:T(8,128)(2,1)S(1)}, bf16[160,512]{1,0:T(8,128)(2,1)S(1)}, u32[]{:S(2)}, u32[]{:S(2)}) collective-permute-start(bf16[160,512]{1,0:T(8,128)(2,1)S(1)} %get-tuple-element.324), channel_id=1, source_target_pairs={{0,8},{1,9},{2,10},{3,11},{4,12},{5,13},{6,14},{7,15},{8,0},{9,1},... | collective-permute-start | bytes 491528 | tf_op jit(solution)/shard_map/ppermute | solution.py:866
  128.1 5.7 %collective-permute-start.24 = (bf16[128,512]{1,0:T(8,128)(2,1)S(1)}, bf16[128,512]{1,0:T(8,128)(2,1)S(1)}, u32[]{:S(2)}, u32[]{:S(2)}) collective-permute-start(bf16[128,512]{1,0:T(8,128)(2,1)S(1)} %get-tuple-element.322), channel_id=1, source_target_pairs={{0,2},{1,3},{2,0},{3,1},{4,6},{5,7},{6,4},{7,5},{8,10},{9,11},{10,... | collective-permute-start | bytes 393224 | tf_op jit(solution)/shard_map/ppermute | solution.py:866
  129.7 5.0 %collective-permute-start.25 = (bf16[128,512]{1,0:T(8,128)(2,1)S(1)}, bf16[128,512]{1,0:T(8,128)(2,1)S(1)}, u32[]{:S(2)}, u32[]{:S(2)}) collective-permute-start(bf16[128,512]{1,0:T(8,128)(2,1)S(1)} %get-tuple-element.323), channel_id=1, source_target_pairs={{0,16},{16,0},{1,17},{17,1},{2,18},{18,2},{3,19},{19,3},{4,20},{20... | collective-permute-start | bytes 393224 | tf_op jit(solution)/shard_map/ppermute | solution.py:866
  132.1 6.9 %collective-permute-start.30 = (bf16[128,512]{1,0:T(8,128)(2,1)S(1)}, bf16[128,512]{1,0:T(8,128)(2,1)S(1)}, u32[]{:S(2)}, u32[]{:S(2)}) collective-permute-start(bf16[128,512]{1,0:T(8,128)(2,1)S(1)} %get-tuple-element.327), channel_id=1, source_target_pairs={{0,2},{1,3},{2,0},{3,1},{4,6},{5,7},{6,4},{7,5},{8,10},{9,11},{10,... | collective-permute-start | bytes 393224 | tf_op jit(solution)/shard_map/ppermute | solution.py:866
  136.6 8.1 %collective-permute-start.28 = (bf16[128,512]{1,0:T(8,128)(2,1)S(1)}, bf16[128,512]{1,0:T(8,128)(2,1)S(1)}, u32[]{:S(2)}, u32[]{:S(2)}) collective-permute-start(bf16[128,512]{1,0:T(8,128)(2,1)S(1)} %get-tuple-element.336), channel_id=1, source_target_pairs={{0,8},{1,9},{2,10},{3,11},{4,12},{5,13},{6,14},{7,15},{8,0},{9,1},... | collective-permute-start | bytes 393224 | tf_op jit(solution)/shard_map/ppermute | solution.py:866
  136.7 4.8 %collective-permute-start.29 = (bf16[80,512]{1,0:T(8,128)(2,1)S(1)}, bf16[80,512]{1,0:T(8,128)(2,1)S(1)}, u32[]{:S(2)}, u32[]{:S(2)}) collective-permute-start(bf16[80,512]{1,0:T(8,128)(2,1)S(1)} %get-tuple-element.337), channel_id=1, source_target_pairs={{0,4},{1,5},{2,6},{3,7},{4,0},{5,1},{6,2},{7,3},{8,12},{9,13},{10,... | collective-permute-start | bytes 245768 | tf_op jit(solution)/shard_map/ppermute | solution.py:866
  139.0 7.8 %collective-permute-start.33 = (bf16[80,512]{1,0:T(8,128)(2,1)S(1)}, bf16[80,512]{1,0:T(8,128)(2,1)S(1)}, u32[]{:S(2)}, u32[]{:S(2)}) collective-permute-start(bf16[80,512]{1,0:T(8,128)(2,1)S(1)} %get-tuple-element.340), channel_id=1, source_target_pairs={{0,8},{1,9},{2,10},{3,11},{4,12},{5,13},{6,14},{7,15},{8,0},{9,1},... | collective-permute-start | bytes 245768 | tf_op jit(solution)/shard_map/ppermute | solution.py:866
  139.7 7.6 %collective-permute-start.20 = (bf16[128,512]{1,0:T(8,128)(2,1)S(1)}, bf16[128,512]{1,0:T(8,128)(2,1)S(1)}, u32[]{:S(2)}, u32[]{:S(2)}) collective-permute-start(bf16[128,512]{1,0:T(8,128)(2,1)S(1)} %shard_map.208.refs_0_), channel_id=1, source_target_pairs={{0,16},{16,0},{1,17},{17,1},{2,18},{18,2},{3,19},{19,3},{4,20},{20... | collective-permute-start | bytes 393224 | tf_op jit(solution)/shard_map/ppermute | solution.py:866
  144.7 5.9 %collective-permute-start.31 = (bf16[128,512]{1,0:T(8,128)(2,1)S(1)}, bf16[128,512]{1,0:T(8,128)(2,1)S(1)}, u32[]{:S(2)}, u32[]{:S(2)}) collective-permute-start(bf16[128,512]{1,0:T(8,128)(2,1)S(1)} %shard_map.215.refs_2_), channel_id=1, source_target_pairs={{0,16},{16,0},{1,17},{17,1},{2,18},{18,2},{3,19},{19,3},{4,20},{20... | collective-permute-start | bytes 393224 | tf_op jit(solution)/shard_map/ppermute | solution.py:866
  145.2 5.5 %collective-permute-start.32 = (bf16[80,512]{1,0:T(8,128)(2,1)S(1)}, bf16[80,512]{1,0:T(8,128)(2,1)S(1)}, u32[]{:S(2)}, u32[]{:S(2)}) collective-permute-start(bf16[80,512]{1,0:T(8,128)(2,1)S(1)} %shard_map.216.refs_4_), channel_id=1, source_target_pairs={{0,16},{16,0},{1,17},{17,1},{2,18},{18,2},{3,19},{19,3},{4,20},{20... | collective-permute-start | bytes 245768 | tf_op jit(solution)/shard_map/ppermute | solution.py:866
  146.8 4.7 %collective-permute-start.34 = (bf16[80,512]{1,0:T(8,128)(2,1)S(1)}, bf16[80,512]{1,0:T(8,128)(2,1)S(1)}, u32[]{:S(2)}, u32[]{:S(2)}) collective-permute-start(bf16[80,512]{1,0:T(8,128)(2,1)S(1)} %shard_map.217.refs_6_), channel_id=1, source_target_pairs={{0,16},{16,0},{1,17},{17,1},{2,18},{18,2},{3,19},{19,3},{4,20},{20... | collective-permute-start | bytes 245768 | tf_op jit(solution)/shard_map/ppermute | solution.py:866
  (1 other events, 3.1 us)
